TPU v7x, 32 devices: a whole 2x2x4 slice. The times are simulated.
32 devices in a mesh: dp: 4 (over y, x), row: 2 (over core), col: 4 (over z).
Axes of the slice: x: 2, y: 2, z: 4, core: 2. Of those that a mesh axis runs over, the one named last changes fastest.
Arguments:
- layer_in: float32 [16, 1024, 768], P(('dp', 'row'), 'col'), may hold values from -6 to 6
- w_qkv: bfloat16 [768, 3, 768], P('row', None, 'col'), may hold values from -0.21875 to 0.21875
- b_qv: float32 [2, 768], P(None, 'col'), may hold values from -1.8 to 1.8
- w_out: bfloat16 [768, 768], P('col', 'row'), may hold values from -0.875 to 0.875
- b_out: float32 [768], replicated, may hold values from -1.8 to 1.8
- ln1_g: float32 [768], replicated, may hold values from 0.1 to 1.9
- ln1_b: float32 [768], replicated, may hold values from -1.8 to 1.8
- ln2_g: float32 [768], replicated, may hold values from 0.1 to 1.9
- ln2_b: float32 [768], replicated, may hold values from -1.8 to 1.8
- w_fc: bfloat16 [768, 3072], P('row', 'col'), may hold values from -0.21875 to 0.21875
- b_fc: float32 [3072], P('col'), may hold values from -1.8 to 1.8
- w_proj: bfloat16 [3072, 768], P('col', 'row'), may hold values from -0.109375 to 0.109375
- b_proj: float32 [768], replicated, may hold values from -1.8 to 1.8
- lengths: int32 [16], P(('dp', 'row')), may hold values from 64 to 1024, as said below
- cotangent: float32 [16, 1024, 768], P(('dp', 'row'), 'col'), may hold values from -6 to 6
Outputs:
- layer_out: float32 [16, 1024, 768], P(('dp', 'row'), 'col')
- grad_input: float32 [16, 1024, 768], P(('dp', 'row'), 'col')
- sample_norms: float32 [16], P(('dp', 'row'))
- grad_w_qkv: float32 [768, 3, 768], P('row', None, 'col')
- grad_b_qv: float32 [2, 768], P(None, 'col')
- grad_w_out: float32 [768, 768], P('col', 'row')
- grad_b_out: float32 [768], replicated
- grad_ln1_g: float32 [768], replicated
- grad_ln1_b: float32 [768], replicated
- grad_ln2_g: float32 [768], replicated
- grad_ln2_b: float32 [768], replicated
- grad_w_fc: float32 [768, 3072], P('row', 'col')
- grad_b_fc: float32 [3072], P('col')
- grad_w_proj: float32 [3072, 768], P('col', 'row')
- grad_b_proj: float32 [768], replicated
Inputs may be any that keep to these rules, and one draw needn't show every extreme that they name: `lengths`: among the 2 sequences of each index pair of dp and row (an aligned block of 2 entries), one has more than 768 real tokens; some sequence has all 1024 slots real.
All inputs are finite; a program needn't handle non-finite values.
Results may differ from a plain program's by a relative error of at most 0.015.
Values may be sent and summed in bfloat16 or wider, within the bound.
A program may use at most 192 MiB of HBM per device.

v0:
```python
import functools

import jax
import jax.numpy as jnp
from jax import lax
from jax.experimental import pallas as pl
from jax.experimental.pallas import tpu as pltpu
from jax.sharding import PartitionSpec as P

MESH = pl.DeviceIdType.MESH
EPSILON = 1e-05
CLIP_BOUND = 1.0
GELU_C = 0.7978845608028654
GELU_A = 0.044715
MASKED = -1e30
HEAD_DIM = 64
QUAD = 4
BF = jnp.bfloat16
F32 = jnp.float32

V_BOUT, V_LN1G, V_LN1B, V_LN2G, V_LN2B, V_BPROJ, V_BQV, V_BFC, V_SQ = 0, 1, 2, 3, 4, 5, 6, 7, 9
V_FACTOR, V_NORM = 12, 13


def dot(a, b):
    return lax.dot_general(a, b, (((1,), (0,)), ((), ())), preferred_element_type=F32)


def dot_t(a, b):
    return lax.dot_general(a, b, (((1,), (1,)), ((), ())), preferred_element_type=F32)


def t_dot(a, b):
    return lax.dot_general(a, b, (((0,), (0,)), ((), ())), preferred_element_type=F32)


def fold8(v):
    return jnp.sum(v.reshape(v.shape[0] // 8, 8, v.shape[1]), axis=0)


def norm_stats(v):
    center = v - jnp.mean(v, axis=-1, keepdims=True)
    inverse = lax.rsqrt(jnp.mean(center * center, axis=-1, keepdims=True) + EPSILON)
    return center * inverse, inverse


def kernel(
    x_in, cot_in, wq_in, wo_in, wf_in, wp_in, misc_in, vec_in,
    lo_out, gi_out, gq_out, go_out, gf_out, gp_out, vec_out, norm_out,
    XR, H, A1, WQ, WO, WF, WP, MISC, QKV, CTX, LSE, KB, ACC,
    PS, PR, A2, M, SL, GF, GA, GCTX, GQKV, DK, DV, LO, GI,
    V8, SQ, VF, VK, VP, VZ,
    GWQ, GWO, GWF, GWP, RQ, RO, RF, RF2, RP, SQW, SOW, SFW, SFW2, SPW, ZQ, ZO, ZF, ZF2, ZP, EQ, EO, EF, EF2, EP,
    ss, rs,
):
    d, row, z = lax.axis_index("dp"), lax.axis_index("row"), lax.axis_index("col")
    k = lax.rem(row, 2)
    dq = d

    def at(plane, core, place):
        return (plane, row - k + core, place)

    zk, zs = z // 2, lax.rem(z, 2)
    L, D = A1.shape
    T = XR.shape[1]
    HC = CTX.shape[1]
    FH = M.shape[1]
    QR, OR_, FR, PR_ = wq_in.shape[1], wo_in.shape[0], wf_in.shape[0], wp_in.shape[0]
    DH = wo_in.shape[1]
    own, other = k * 2 * T, (1 - k) * 2 * T

    def mo(v, n):
        return pl.multiple_of(v, n)

    def when(cond, f):
        if cond is True:
            f()
        else:
            pl.when(cond)(f)

    n_send = [0]
    n_recv = [0]
    pending = []

    def new_send():
        n_send[0] += 1
        assert n_send[0] <= ss.shape[0]
        return n_send[0] - 1

    def new_recv(n):
        n_recv[0] += n
        assert n_recv[0] <= rs.shape[0]
        return n_recv[0] - n

    def send(src, dst, rsem, dev, cond=True):
        sem = new_send()

        def make():
            return pltpu.make_async_remote_copy(
                src(), dst(), ss.at[sem], rs.at[rsem], device_id=dev, device_id_type=MESH
            )

        when(cond, lambda: make().start())
        pending.append((cond, make))

    def local(src, dst, rsem, cond=True):
        when(cond, lambda: pltpu.make_async_copy(src(), dst(), rs.at[rsem]).start())

    def arrive(dst, rsem, cond=True):
        def f():
            pltpu.make_async_remote_copy(
                dst(), dst(), ss.at[0], rs.at[rsem], device_id=at(d, k, z), device_id_type=MESH
            ).wait_recv()

        when(cond, f)

    def arrive_local(dst, rsem, cond=True):
        when(cond, lambda: pltpu.make_async_copy(dst(), dst(), rs.at[rsem]).wait())

    mate = at(d, 1 - k, z)
    quad = [at(d ^ j, k, z) for j in (1, 2, 3)]

    barrier = pltpu.get_barrier_semaphore()
    line = [at(d, k, z ^ j) for j in (1, 2, 3)] + [at(d, 1 - k, z ^ j) for j in (0, 1, 2, 3)]
    for dev in quad + line:
        pl.semaphore_signal(barrier, inc=1, device_id=dev, device_id_type=MESH)
    pl.semaphore_wait(barrier, len(quad) + len(line))

    def line_send(src, dst):
        base = new_recv(2)
        for i in range(2):
            mine = (zk == k) & (2 * k + i == z)
            send(lambda i=i: src(i), lambda: dst(zs), base + zs, at(d, zk, 2 * k + i), jnp.logical_not(mine))
            local(lambda i=i: src(i), lambda: dst(zs), base + zs, mine)
        return base

    def line_wait(dst, base, i):
        mine = (zk == k) & (2 * k + i == z)
        arrive(lambda: dst(i), base + i, jnp.logical_not(mine))
        arrive_local(lambda: dst(i), base + i, mine)

    away = [2 * k + cs != z for cs in range(2)]
    near_mate = [[(2 * k + cs == z) & (k != r) for r in range(2)] for cs in range(2)]
    near_self = [[(2 * k + cs == z) & (k == r) for r in range(2)] for cs in range(2)]

    class Weight:
        def __init__(self, src, src_quarter, piece, full, slab):
            self.src, self.src_quarter, self.piece, self.full, self.slab = src, src_quarter, piece, full, slab
            self.zsem, self.xsem = new_recv(4), new_recv(8)

        def push(self):
            sem = self.zsem + zs * 2 + k
            for j in (1, 2, 3):
                send(self.src_quarter, lambda: self.piece(zs, k, dq), sem, at(d, zk, z ^ j))
            send(self.src, lambda: self.full(zs, k), sem, mate, zk != k)
            local(self.src, lambda: self.full(zs, k), sem, zk == k)

        def forward(self):
            for cs in range(2):
                for r in range(2):
                    sem = self.zsem + cs * 2 + r
                    arrive(lambda: self.piece(cs, r, dq), sem, away[cs])
                    arrive(lambda: self.full(cs, r), sem, near_mate[cs][r])
                    arrive_local(lambda: self.full(cs, r), sem, near_self[cs][r])
                mine = lambda cs=cs: self.slab(cs, dq)
                for j in (1, 2):
                    send(mine, mine, self.xsem + cs * 4 + j - 1, quad[j - 1], away[cs])

        def relay(self):
            for cs in range(2):
                for j in (1, 2):
                    arrive(lambda: self.slab(cs, dq ^ j), self.xsem + cs * 4 + j - 1, away[cs])
                    half = lambda cs=cs, j=j: self.piece(cs, j - 1, dq ^ j)
                    send(half, half, self.xsem + cs * 4 + 1 + j, quad[2 - j], away[cs])

        def ready(self):
            for cs in range(2):
                for j in (1, 2):
                    arrive(lambda: self.piece(cs, j - 1, dq ^ 3), self.xsem + cs * 4 + 1 + j, away[cs])

    q48, o48, f96, p192 = QR // QUAD, OR_ // QUAD, FR // QUAD, PR_ // QUAD

    def cols(r):
        return pl.ds(mo(r * DH, 128), DH)

    w_qkv = Weight(
        lambda: wq_in,
        lambda: wq_in.at[:, pl.ds(mo(dq * q48, 16), q48), :],
        lambda cs, r, q: WQ.at[:, pl.ds(mo(cs * QR + q * q48, 16), q48), cols(r)],
        lambda cs, r: WQ.at[:, pl.ds(mo(cs * QR, 16), QR), cols(r)],
        lambda cs, q: WQ.at[:, pl.ds(mo(cs * QR + q * q48, 16), q48), :],
    )
    w_out = Weight(
        lambda: wo_in,
        lambda: wo_in.at[pl.ds(mo(dq * o48, 16), o48), :],
        lambda cs, r, q: WO.at[pl.ds(mo(cs * OR_ + q * o48, 16), o48), cols(r)],
        lambda cs, r: WO.at[pl.ds(mo(cs * OR_, 16), OR_), cols(r)],
        lambda cs, q: WO.at[pl.ds(mo(cs * OR_ + q * o48, 16), o48), :],
    )
    FC = wf_in.shape[1]

    def fc_part(at0, n):
        return Weight(
            lambda: wf_in.at[:, pl.ds(at0, n)],
            lambda: wf_in.at[pl.ds(mo(dq * f96, 16), f96), pl.ds(at0, n)],
            lambda cs, r, q: WF.at[r, pl.ds(mo(q * f96, 16), f96), pl.ds(mo(cs * FC + at0, 128), n)],
            lambda cs, r: WF.at[r, :, pl.ds(mo(cs * FC + at0, 128), n)],
            lambda cs, q: WF.at[:, pl.ds(mo(q * f96, 16), f96), pl.ds(mo(cs * FC + at0, 128), n)],
        )

    def proj_part(at0, n):
        n4 = n // QUAD
        return Weight(
            lambda: wp_in.at[pl.ds(at0, n), :],
            lambda: wp_in.at[pl.ds(mo(at0 + dq * n4, 16), n4), :],
            lambda cs, r, q: WP.at[pl.ds(mo(cs * PR_ + at0 + q * n4, 16), n4), cols(r)],
            lambda cs, r: WP.at[pl.ds(mo(cs * PR_ + at0, 16), n), cols(r)],
            lambda cs, q: WP.at[pl.ds(mo(cs * PR_ + at0 + q * n4, 16), n4), :],
        )

    first = FC // 3
    w_fc, w_fc2 = fc_part(0, first), fc_part(first, FC - first)
    w_proj, w_proj2 = proj_part(0, first), proj_part(first, FC - first)

    misc_sem = new_recv(8)
    for dev in line:
        send(lambda: misc_in, lambda: MISC.at[k, z], misc_sem + k * 4 + z, dev)
    local(lambda: misc_in, lambda: MISC.at[k, z], misc_sem + k * 4 + z)
    w_qkv.push()
    x_sem = line_send(lambda i: x_in.at[i], lambda i: XR.at[i])

    V8[...] = jnp.zeros_like(V8)
    SQ[...] = jnp.zeros_like(SQ)

    vec = lambda i: vec_in[i : i + 1, :]
    b_out, ln1_g, ln1_b, ln2_g, ln2_b, b_proj = (vec(i) for i in range(6))

    w_qkv.forward()
    w_qkv.relay()

    RB = 32
    a1_sem = new_recv(2)

    def rows_of(base, i, n):
        return pl.ds(mo(base + i * n, 16), n)

    for s in range(2):
        line_wait(lambda i: XR.at[i], x_sem, s)

        def first_norm(i, c):
            scaled, _ = norm_stats(XR[s, rows_of(0, i, RB), :].astype(F32))
            A1[rows_of(own + s * T, i, RB), :] = (scaled * ln1_g + ln1_b).astype(BF)
            return c

        lax.fori_loop(0, T // RB, first_norm, 0)
        mine = lambda s=s: A1.at[pl.ds(mo(own + s * T, 16), T), :]
        send(mine, mine, a1_sem + s, mate)

    for r in range(2):
        for c in range(4):
            here = (k == r) & (z == c)
            arrive(lambda: MISC.at[r, c], misc_sem + r * 4 + c, jnp.logical_not(here))
            arrive_local(lambda: MISC.at[r, c], misc_sem + r * 4 + c, here)
    pair_misc = MISC[0, 2 * k] + MISC[0, 2 * k + 1]
    bias_q, bias_v = pair_misc[1:2, :HC], pair_misc[1:2, HC:]
    length = MISC[zk, 0, pl.ds(2 + zs, 1), :][:, 0:1]

    w_qkv.ready()

    def project(i, c):
        rows = rows_of(0, lax.rem(2 * k + i, 4), T)
        a = A1[rows, :]
        QKV[0, rows, :] = ((dot_t(a, WQ[0]) + bias_q).astype(BF).astype(F32) * (HEAD_DIM**-0.5)).astype(BF)
        QKV[1, rows, :] = dot_t(a, WQ[1]).astype(BF)
        QKV[2, rows, :] = (dot_t(a, WQ[2]) + bias_v).astype(BF)
        return c

    lax.fori_loop(0, 2, project, 0)
    for s in range(2):
        arrive(lambda: A1.at[pl.ds(mo(other + s * T, 16), T), :], a1_sem + s)
    for w in (w_out, w_fc, w_fc2, w_proj, w_proj2):
        w.push()
    cot_sem = line_send(lambda i: cot_in.at[i], lambda i: GF.at[pl.ds(mo(z * T, 16), T), :])
    lax.fori_loop(2, 4, project, 0)

    key_place = lax.broadcasted_iota(jnp.int32, (L, 128), 0).astype(F32)
    KB[...] = jnp.where(key_place < length, 0.0, MASKED)

    QB = T
    NQ = L // QB
    low_lane = lax.broadcasted_iota(jnp.int32, (1, 128), 1) < HEAD_DIM
    low_row = lax.broadcasted_iota(jnp.int32, (128, 1), 0) < HEAD_DIM
    diag = lax.broadcasted_iota(jnp.int32, (QB, QB), 0) <= lax.broadcasted_iota(jnp.int32, (QB, QB), 1)

    def keep_lane(v, h):
        return jnp.where(low_lane if h == 0 else jnp.logical_not(low_lane), v, jnp.zeros_like(v))

    def scores_t(kp, qm, qb):
        kv = (qb + 1) * QB
        s = dot_t(kp[:kv], qm)
        kb = KB[0:kv, :]
        s = s + jnp.concatenate([kb] * (QB // 128), axis=1)
        last = jnp.where(diag, s[kv - QB :], MASKED)
        if qb == 0:
            return last
        return jnp.concatenate([s[: kv - QB], last], axis=0)

    def attend(p):
        lanes = pl.ds(mo(p * 128, 128), 128)
        kp, vp = QKV[1, :, lanes], QKV[2, :, lanes]
        vt = vp.T
        for qb in range(NQ):
            kv = (qb + 1) * QB
            qp = QKV[0, qb * QB : kv, lanes]
            parts = []
            for h in range(2):
                s = scores_t(kp, keep_lane(qp, h), qb)
                top = jnp.max(s, axis=0, keepdims=True)
                e = jnp.exp(s - top)
                total = jnp.sum(e, axis=0, keepdims=True)
                LSE[pl.ds(2 * p + h, 1), qb * QB : kv] = top + jnp.log(total)
                parts.append(dot(vt[:, :kv], e.astype(BF)) / total)
            CTX[qb * QB : kv, lanes] = jnp.where(low_row, parts[0], parts[1]).T.astype(BF)

    def attend_step(p, c):
        @pl.when(p == 1)
        def _():
            w_out.forward()
            w_fc.forward()

        @pl.when(p == 2)
        def _():
            w_out.relay()
            w_fc.relay()

        attend(p)
        return c

    lax.fori_loop(0, HC // 128, attend_step, 0)
    w_fc2.forward()

    def split_sum(n, product, sums=None):
        base = new_recv(2)
        for s in range(2):
            PS[n, s] = product(pl.ds(mo(other + s * T, 16), T)).astype(BF)
            send(lambda s=s: PS.at[n, s], lambda s=s: PR.at[n, s], base + s, mate)

        def keep(s, c):
            ACC[s] = product(pl.ds(mo(own + s * T, 16), T))
            return c

        lax.fori_loop(0, 2, keep, 0)
        return base

    def split_wait(n, base, s):
        arrive(lambda: PR.at[n, s], base + s)

    w_out.ready()
    ex = split_sum(0, lambda rows: dot(CTX[rows, :], WO[...]))
    w_fc2.relay()
    w_proj.forward()
    a2_sem = new_recv(2)
    for s in range(2):
        split_wait(0, ex, s)

        def second_norm(i, c):
            rows = rows_of(0, i, RB)
            h = XR[s, rows, :].astype(F32) + ACC[s, rows, :] + PR[0, s, rows, :].astype(F32) + b_out
            H[s, rows, :] = h
            scaled, _ = norm_stats(h)
            A2[rows_of(own + s * T, i, RB), :] = (scaled * ln2_g + ln2_b).astype(BF)
            return c

        lax.fori_loop(0, T // RB, second_norm, 0)
        mine = lambda s=s: A2.at[pl.ds(mo(own + s * T, 16), T), :]
        send(mine, mine, a2_sem + s, mate)

    VF[...] = jnp.concatenate([MISC[0, 2 * k, 0:1, :], MISC[0, 2 * k + 1, 0:1, :]], axis=1)

    def hidden(start, width):
        def body(i, c):
            rows = rows_of(0, lax.rem(2 * k + i // 2, 4), T)
            cs = pl.ds(mo(lax.rem(i, 2) * FC + start, 128), width)
            u = dot(A2[rows, :], WF[:, :, cs].reshape(D, width)) + VF[:, cs]
            t = jnp.tanh(GELU_C * (u + GELU_A * u * u * u))
            M[rows, cs] = (0.5 * u * (1.0 + t)).astype(BF)
            SL[rows, cs] = (
                0.5 * (1.0 + t) + 0.5 * u * (1.0 - t * t) * GELU_C * (1.0 + 3.0 * GELU_A * u * u)
            ).astype(BF)
            return c

        return body

    w_fc.ready()
    lax.fori_loop(0, 4, hidden(0, first), 0)
    for s in range(2):
        arrive(lambda: A2.at[pl.ds(mo(other + s * T, 16), T), :], a2_sem + s)
    lax.fori_loop(4, 8, hidden(0, first), 0)
    w_proj2.forward()
    w_proj.relay()
    w_fc2.ready()
    lax.fori_loop(0, 8, hidden(first, FC - first), 0)
    w_proj2.relay()
    w_proj.ready()
    w_proj2.ready()
    ex = split_sum(1, lambda rows: dot(M[rows, :], WP[...]))

    gf_sem = new_recv(2)
    for s in range(2):
        line_wait(lambda i: GF.at[pl.ds(mo(own + i * T, 16), T), :], cot_sem, s)

        def mask_rows(i, c):
            rows = rows_of(own + s * T, i, RB)
            place = (lax.broadcasted_iota(jnp.int32, (RB, 1), 0) + (own + s * T + i * RB)).astype(F32)
            g = jnp.where(place < length, GF[rows, :].astype(F32), 0.0)
            GF[rows, :] = g.astype(BF)
            V8[V_BPROJ] += fold8(g)
            return c

        lax.fori_loop(0, T // RB, mask_rows, 0)
        mine = lambda s=s: GF.at[pl.ds(mo(own + s * T, 16), T), :]
        send(mine, mine, gf_sem + s, mate)

    for s in range(2):
        split_wait(1, ex, s)

        def output_rows(i, c):
            rows = rows_of(0, i, RB)
            LO[s, rows, :] = (H[s, rows, :] + ACC[s, rows, :] + PR[1, s, rows, :].astype(F32) + b_proj).astype(BF)
            return c

        lax.fori_loop(0, T // RB, output_rows, 0)
    lo_sem = line_send(lambda i: LO.at[i], lambda i: lo_out.at[i])

    for s in range(2):
        arrive(lambda: GF.at[pl.ds(mo(other + s * T, 16), T), :], gf_sem + s)

    class Part:
        def __init__(self, quarter, R, S, Z, E, pieces, place):
            self.quarter, self.R, self.S, self.Z, self.E = quarter, R, S, Z, E
            self.pieces, self.place = pieces, place
            self.raw, self.zsem, self.end = new_recv(3), new_recv(4), new_recv(4)

        def spread(self):
            for j in (1, 2, 3):
                send(lambda j=j: self.quarter(dq ^ j), lambda j=j: self.R.at[j - 1], self.raw + j - 1, quad[j - 1])

        def reduce(self):
            for j in (1, 2, 3):
                arrive(lambda: self.R.at[j - 1], self.raw + j - 1)
            G, (_, n, width) = self.quarter(dq), self.S.shape
            wide = lambda f: f if width <= D else jnp.concatenate([f] * (width // D), axis=1)
            factors = [wide(VP[dq ^ j, V_FACTOR : V_FACTOR + 1, :]) for j in range(QUAD)]
            steps = n // 16

            def add(i, c):
                a, rows = i // steps, pl.ds(mo(lax.rem(i, steps) * 16, 16), 16)
                v = G[a, rows, :].astype(F32) * factors[0]
                for j in (1, 2, 3):
                    v = v + self.R[j - 1, a, rows, :].astype(F32) * factors[j]
                self.S[a, rows, :] = v.astype(BF)
                return c

            lax.fori_loop(0, 2 * steps, add, 0)
            for cs in range(2):
                for r in range(2):
                    mine = (r == k) & (2 * k + cs == z)
                    piece = lambda cs=cs, r=r: self.pieces(cs, r)
                    send(piece, lambda: self.Z.at[z], self.zsem + z, at(d, r, 2 * k + cs), jnp.logical_not(mine))
                    local(piece, lambda: self.Z.at[z], self.zsem + z, mine)

        def finish(self):
            for c in range(4):
                here = (zk == k) & (z == c)
                arrive(lambda: self.Z.at[c], self.zsem + c, jnp.logical_not(here))
                arrive_local(lambda: self.Z.at[c], self.zsem + c, here)
            Z = self.Z
            self.E[...] = (
                Z[0].astype(F32) + Z[1].astype(F32) + Z[2].astype(F32) + Z[3].astype(F32)
            ).astype(BF)
            for j in (1, 2, 3):
                send(lambda: self.E, lambda: self.place(dq), self.end + j, quad[j - 1])
            local(lambda: self.E, lambda: self.place(dq), self.end)

        def done(self):
            arrive_local(lambda: self.place(dq), self.end)
            for j in (1, 2, 3):
                arrive(lambda: self.place(dq ^ j), self.end + j)

    g_proj = Part(
        lambda q: GWP.at[:, pl.ds(mo(q * p192, 16), p192), :], RP, SPW, ZP, EP,
        lambda cs, r: SPW.at[cs, :, cols(r)],
        lambda q: gp_out.at[pl.ds(mo(q * p192, 16), p192), :],
    )
    g_out = Part(
        lambda q: GWO.at[:, pl.ds(mo(q * o48, 16), o48), :], RO, SOW, ZO, EO,
        lambda cs, r: SOW.at[cs, :, cols(r)],
        lambda q: go_out.at[pl.ds(mo(q * o48, 16), o48), :],
    )

    def fc_grad(R, S, Z, E, start, n):
        return Part(
            lambda q: GWF.at[:, pl.ds(mo(start + q * n, 16), n), :], R, S, Z, E,
            lambda cs, r: S.at[r, :, pl.ds(mo(cs * FC, 128), FC)],
            lambda q: gf_out.at[pl.ds(mo(start + q * n, 16), n), :],
        )

    g_fc = fc_grad(RF, SFW, ZF, EF, 0, 128 // QUAD)
    g_fc2 = fc_grad(RF2, SFW2, ZF2, EF2, 128, (FR - 128) // QUAD)

    def qkv_grad(i):
        return Part(
            lambda q: GWQ.at[i, :, pl.ds(mo(q * q48, 16), q48), :], RQ.at[i], SQW.at[i], ZQ.at[i], EQ.at[i],
            lambda cs, r: SQW.at[i, cs, :, cols(r)],
            lambda q: gq_out.at[i, pl.ds(mo(q * q48, 16), q48), :],
        )

    g_qkv = [qkv_grad(i) for i in range(3)]

    def grad_proj(i, c):
        cs = pl.ds(mo(i * 256, 128), 256)
        g = t_dot(M[:, cs], GF[...])
        SQ[...] += fold8(g * g)
        GWP[i // 3, pl.ds(mo(lax.rem(i, 3) * 256, 16), 256), :] = g.astype(BF)
        return c

    lax.fori_loop(0, FH // 256, grad_proj, 0)
    g_proj.spread()

    NB = 512
    NN = FH // NB

    def grad_hidden(i, c):
        rows = rows_of(0, i // NN, T)
        cs = pl.ds(mo(lax.rem(i, NN) * NB, 128), NB)
        g = dot_t(GF[rows, :], WP[cs, :]) * SL[rows, cs].astype(F32)
        low = g.astype(BF)
        SL[rows, cs] = low
        VF[:, cs] = jnp.where(i < NN, 0.0, VF[:, cs]) + jnp.sum(low.astype(F32), axis=0, keepdims=True)
        return c

    lax.fori_loop(0, 4 * NN, grad_hidden, 0)
    ex = split_sum(2, lambda rows: dot_t(SL[rows, :], WF[...].reshape(D, FH)))

    ga_sem = new_recv(2)
    for s in range(2):
        split_wait(2, ex, s)

        def second_back(i, c):
            rows = rows_of(0, i, RB)
            full = rows_of(own + s * T, i, RB)
            up = ACC[s, rows, :] + PR[2, s, rows, :].astype(F32)
            scaled, inverse = norm_stats(H[s, rows, :])
            through = up * ln2_g
            V8[V_LN2G] += fold8(up * scaled)
            V8[V_LN2B] += fold8(up)
            g = GF[full, :].astype(F32) + inverse * (
                through
                - jnp.mean(through, axis=-1, keepdims=True)
                - scaled * jnp.mean(through * scaled, axis=-1, keepdims=True)
            )
            V8[V_BOUT] += fold8(g)
            H[s, rows, :] = g
            GA[full, :] = g.astype(BF)
            return c

        lax.fori_loop(0, T // RB, second_back, 0)
        mine = lambda s=s: GA.at[pl.ds(mo(own + s * T, 16), T), :]
        send(mine, mine, ga_sem + s, mate)
    for s in range(2):
        arrive(lambda: GA.at[pl.ds(mo(other + s * T, 16), T), :], ga_sem + s)

    def grad_context(i, c):
        rows = rows_of(0, i, T)
        GCTX[rows, :] = dot_t(GA[rows, :], WO[...]).astype(BF)
        return c

    lax.fori_loop(0, 4, grad_context, 0)
    half = HC // 2
    for cs in range(HC // 128):
        g = t_dot(CTX[:, cs * 128 : (cs + 1) * 128], GA[...])
        SQ[...] += fold8(g * g)
        low = g.astype(BF)
        lo_row = cs * 128
        if lo_row + 128 <= half:
            GWO[0, lo_row : lo_row + 128, :] = low
        elif lo_row >= half:
            GWO[1, lo_row - half : lo_row - half + 128, :] = low
        else:
            GWO[0, lo_row:half, :] = low[: half - lo_row]
            GWO[1, : lo_row + 128 - half, :] = low[half - lo_row :]
    g_out.spread()

    def grad_fc(i, c):
        block = lax.rem(i, 2) * 3 + i // 2
        cs = pl.ds(mo(block * 128, 128), 128)
        g = t_dot(A2[:, cs], SL[...])
        q = fold8(g * g)
        SQ[...] += q[:, :D] + q[:, D:]
        GWF[lax.rem(i, 2), pl.ds(mo(i // 2 * 128, 16), 128), :] = g.astype(BF)
        return c

    lax.fori_loop(0, 2, grad_fc, 0)
    g_fc.spread()

    def attend_back(p):
        lanes = pl.ds(mo(p * 128, 128), 128)
        kp, vp = QKV[1, :, lanes], QKV[2, :, lanes]
        kt = kp.T
        DK[...] = jnp.zeros_like(DK)
        DV[...] = jnp.zeros_like(DV)
        for qb in range(NQ):
            kv = (qb + 1) * QB
            qp = QKV[0, qb * QB : kv, lanes]
            do = GCTX[qb * QB : kv, lanes]
            dqt = []
            for h in range(2):
                qm, dm = keep_lane(qp, h), keep_lane(do, h)
                pt = jnp.exp(scores_t(kp, qm, qb) - LSE[pl.ds(2 * p + h, 1), qb * QB : kv])
                gp = dot_t(vp[:kv], dm)
                both = pt * gp
                gs = (both - pt * jnp.sum(both, axis=0, keepdims=True)).astype(BF)
                DV[0:kv, :] += dot(pt.astype(BF), dm)
                DK[0:kv, :] += dot(gs, qm)
                dqt.append(dot(kt[:, :kv], gs))
            GQKV[0, qb * QB : kv, lanes] = (
                jnp.where(low_row, dqt[0], dqt[1]).T * (HEAD_DIM**-0.5)
            ).astype(BF)
        GQKV[1, :, lanes] = DK[...].astype(BF)
        GQKV[2, :, lanes] = DV[...].astype(BF)

    def attend_back_step(p, c):
        attend_back(p)
        return c

    lax.fori_loop(0, HC // 128, attend_back_step, 0)

    def grad_norm_in(rows):
        return dot(GQKV[0, rows, :], WQ[0]) + dot(GQKV[1, rows, :], WQ[1]) + dot(GQKV[2, rows, :], WQ[2])

    ex = split_sum(3, grad_norm_in)
    lax.fori_loop(2, D // 128, grad_fc, 0)
    for s in range(2):
        split_wait(3, ex, s)

        def first_back(i, c):
            rows = rows_of(0, i, RB)
            up = ACC[s, rows, :] + PR[3, s, rows, :].astype(F32)
            scaled, inverse = norm_stats(XR[s, rows, :].astype(F32))
            through = up * ln1_g
            V8[V_LN1G] += fold8(up * scaled)
            V8[V_LN1B] += fold8(up)
            g = H[s, rows, :] + inverse * (
                through
                - jnp.mean(through, axis=-1, keepdims=True)
                - scaled * jnp.mean(through * scaled, axis=-1, keepdims=True)
            )
            GI[s, rows, :] = g.astype(BF)
            return c

        lax.fori_loop(0, T // RB, first_back, 0)

    gi_sem = line_send(lambda i: GI.at[i], lambda i: gi_out.at[i])

    def grad_qkv(i, c):
        g = t_dot(GQKV[i], A1[...])
        SQ[...] += fold8(g * g)
        low = g.astype(BF)
        GWQ[i, 0] = low[:half]
        GWQ[i, 1] = low[half:]
        return c

    lax.fori_loop(0, 3, grad_qkv, 0)
    VK[k] = jnp.zeros(VK.shape[1:], F32)
    for i in range(6):
        VK[k, i : i + 1, :] = jnp.sum(V8[i], axis=0, keepdims=True)
    VK[k, V_BQV : V_BQV + 1, :] = jnp.concatenate(
        [jnp.sum(GQKV[i].astype(F32), axis=0, keepdims=True) for i in (0, 2)], axis=1
    )
    VK[k, V_BFC : V_BFC + 1, :] = VF[:, :D]
    VK[k, V_BFC + 1 : V_BFC + 2, :] = VF[:, D:]
    VK[k, V_SQ : V_SQ + 1, :] = jnp.sum(SQ[...], axis=0, keepdims=True)
    vk_sem = new_recv(1)
    send(lambda: VK.at[k], lambda: VK.at[k], vk_sem, mate)
    arrive(lambda: VK.at[1 - k], vk_sem)
    va, vb = VK[0], VK[1]
    pack = jnp.concatenate([va[0:6] + vb[0:6], va[6:9], vb[6:9]], axis=0)
    squares = jnp.sum(jnp.sum(pack * pack, axis=0, keepdims=True) + va[9:10] + vb[9:10], axis=1, keepdims=True)
    norm = jnp.sqrt(squares)
    factor = CLIP_BOUND / jnp.maximum(norm, CLIP_BOUND)
    wide = lambda v: jnp.broadcast_to(v, (1, D))
    VP[dq] = jnp.concatenate([pack, wide(factor), wide(norm), jnp.zeros((2, D), F32)], axis=0)
    vp_sem = new_recv(3)
    for j in (1, 2, 3):
        send(lambda: VP.at[dq], lambda: VP.at[dq], vp_sem + j - 1, quad[j - 1])
    for part in (g_fc2, *g_qkv):
        part.spread()

    for j in (1, 2, 3):
        arrive(lambda: VP.at[dq ^ j], vp_sem + j - 1)

    total = jnp.zeros((12, D), F32)
    for q in range(QUAD):
        total = total + VP[q, 0:12, :] * VP[q, V_FACTOR : V_FACTOR + 1, :]
    VZ[z] = jnp.concatenate([total, VP[dq, V_FACTOR:, :]], axis=0)
    vz_sem = new_recv(3)
    for j in (1, 2, 3):
        send(lambda: VZ.at[z], lambda: VZ.at[z], vz_sem + j - 1, at(d, k, z ^ j))

    order = [g_proj, g_out, g_fc, g_fc2, *g_qkv]
    for i, part in enumerate(order):
        part.reduce()
        if i >= 2:
            order[i - 2].finish()
    for part in order[-2:]:
        part.finish()

    for j in (1, 2, 3):
        arrive(lambda: VZ.at[z ^ j], vz_sem + j - 1)
    vec_out[...] = (VZ[0] + VZ[1] + VZ[2] + VZ[3])[0:12]
    for c in range(4):
        norm_out[c : c + 1, :] = VZ[c, V_NORM : V_NORM + 1, 0:128]

    for part in order:
        part.done()
    for i in range(2):
        line_wait(lambda i: lo_out.at[i], lo_sem, i)
        line_wait(lambda i: gi_out.at[i], gi_sem, i)
    for cond, make in pending:
        when(cond, lambda: make().wait_send())


def shards(
    layer_in, w_qkv, b_qv, w_out, b_out, ln1_g, ln1_b, ln2_g, ln2_b, w_fc, b_fc, w_proj, b_proj, lengths, cotangent
):
    E, T, D = layer_in.shape
    n_col, n_row = lax.axis_size("col"), lax.axis_size("row")
    assert lax.axis_size("dp") == QUAD and n_col == 4 and n_row % 2 == 0
    pairs = n_row // 2
    r = lax.axis_index("row")
    core = lax.rem(r, 2)
    half_rows = w_fc.shape[0] * pairs

    def halves(w, axis):
        if pairs == 1:
            return w
        whole = lax.all_gather(w, "row", axis=axis, tiled=True)
        return lax.dynamic_slice_in_dim(whole, core * half_rows, half_rows, axis)

    w_qkv, w_out, w_fc, w_proj = halves(w_qkv, 0), halves(w_out, 1), halves(w_fc, 0), halves(w_proj, 1)
    L = T * n_col
    HQ = w_qkv.shape[2]
    HC = HQ * n_col // 2
    FQ = w_fc.shape[1]
    FH = FQ * n_col // 2
    DH = w_fc.shape[0]
    c = lax.axis_index("col")

    zero = jnp.zeros_like(b_qv)
    even = lax.rem(c, 2) == 0
    both = jnp.where(
        even, jnp.concatenate([b_qv, zero], axis=1), jnp.concatenate([zero, b_qv], axis=1)
    ).reshape(1, 2 * HC)
    misc = jnp.concatenate(
        [
            b_fc[None, :],
            both,
            jnp.broadcast_to(lengths.astype(F32)[:, None], (E, D)),
            jnp.zeros((4, D), F32),
        ],
        axis=0,
    )
    vecs = jnp.stack([b_out, ln1_g, ln1_b, ln2_g, ln2_b, b_proj, b_proj, b_proj])
    wq_t = jnp.transpose(w_qkv, (1, 2, 0))
    q48, o48, p192 = HQ // QUAD, HQ // QUAD, FQ // QUAD
    fa, fb = 128 // QUAD, (DH - 128) // QUAD

    anyspec = pl.BlockSpec(memory_space=pl.ANY)
    vm = pl.BlockSpec(memory_space=pltpu.VMEM)
    V = pltpu.VMEM
    outs = pl.pallas_call(
        kernel,
        name="layer",
        out_shape=(
            jax.ShapeDtypeStruct((E, T, D), BF),
            jax.ShapeDtypeStruct((E, T, D), BF),
            jax.ShapeDtypeStruct((3, HQ, DH), BF),
            jax.ShapeDtypeStruct((HQ, DH), BF),
            jax.ShapeDtypeStruct((DH, FQ), BF),
            jax.ShapeDtypeStruct((FQ, DH), BF),
            jax.ShapeDtypeStruct((12, D), F32),
            jax.ShapeDtypeStruct((8, 128), F32),
        ),
        in_specs=[anyspec] * 7 + [vm],
        out_specs=(anyspec,) * 6 + (vm, vm),
        scratch_shapes=[
            V((2, T, D), BF),
            V((2, T, D), F32),
            V((L, D), BF),
            V((3, HC, D), BF),
            V((HC, D), BF),
            V((2, DH, FH), BF),
            V((FH, D), BF),
            V((2, n_col, 8, D), F32),
            V((3, L, HC), BF),
            V((L, HC), BF),
            V((8, L), F32),
            V((L, 128), F32),
            V((2, T, D), F32),
            V((4, 2, T, D), BF),
            V((4, 2, T, D), BF),
            V((L, D), BF),
            V((L, FH), BF),
            V((L, FH), BF),
            V((L, D), BF),
            V((L, D), BF),
            V((L, HC), BF),
            V((3, L, HC), BF),
            V((L, 128), F32),
            V((L, 128), F32),
            V((2, T, D), BF),
            V((2, T, D), BF),
            V((6, 8, D), F32),
            V((8, D), F32),
            V((1, FH), F32),
            V((2, 16, D), F32),
            V((QUAD, 16, D), F32),
            V((n_col, 16, D), F32),
            V((3, 2, HQ, D), BF),
            V((2, HQ, D), BF),
            V((2, DH, FH), BF),
            V((2, FQ, D), BF),
            V((3, 3, 2, q48, D), BF),
            V((3, 2, o48, D), BF),
            V((3, 2, fa, FH), BF),
            V((3, 2, fb, FH), BF),
            V((3, 2, p192, D), BF),
            V((3, 2, q48, D), BF),
            V((2, o48, D), BF),
            V((2, fa, FH), BF),
            V((2, fb, FH), BF),
            V((2, p192, D), BF),
            V((3, 4, q48, DH), BF),
            V((4, o48, DH), BF),
            V((4, fa, FQ), BF),
            V((4, fb, FQ), BF),
            V((4, p192, DH), BF),
            V((3, q48, DH), BF),
            V((o48, DH), BF),
            V((fa, FQ), BF),
            V((fb, FQ), BF),
            V((p192, DH), BF),
            pltpu.SemaphoreType.DMA((200,)),
            pltpu.SemaphoreType.DMA((200,)),
        ],
        compiler_params=pltpu.CompilerParams(
            collective_id=0, has_side_effects=True, vmem_limit_bytes=63 * 2**20
        ),
    )(layer_in.astype(BF), cotangent.astype(BF), wq_t, w_out, w_fc, w_proj, misc, vecs)
    lo, gi, gq, go, gf, gp, vec, norms = outs
    lo, gi, gq, go, gf, gp = (v.astype(F32) for v in (lo, gi, gq, go, gf, gp))
    gq = jnp.transpose(gq, (2, 0, 1))
    if pairs > 1:
        groups = [[2 * p + q for p in range(pairs)] for q in range(2)]
        cores = [[2 * p, 2 * p + 1] for p in range(pairs)]
        gq, go, gf, gp, vec = (
            lax.psum(v, "row", axis_index_groups=groups) for v in (gq, go, gf, gp, vec)
        )

        def share(v, axis):
            whole = lax.all_gather(v, "row", axis=axis, tiled=True, axis_index_groups=cores)
            part = whole.shape[axis] // n_row
            return lax.dynamic_slice_in_dim(whole, r * part, part, axis)

        gq, go, gf, gp = share(gq, 0), share(go, 1), share(gf, 0), share(gp, 1)
    sample_norms = lax.dynamic_slice_in_dim(norms[:, 0], 2 * core, 2, 0)
    row = 6 + 3 * (c // 2)
    part = lax.rem(c, 2)
    bqv = lax.dynamic_slice(vec, (row, 0), (1, D)).reshape(2, HC)
    grad_bqv = lax.dynamic_slice(bqv, (0, part * HQ), (2, HQ))
    grad_bfc = lax.dynamic_slice(vec, (row + 1 + part, 0), (1, D))[0]
    return (
        lo, gi, sample_norms, gq, grad_bqv, go,
        vec[V_BOUT], vec[V_LN1G], vec[V_LN1B], vec[V_LN2G], vec[V_LN2B],
        gf, grad_bfc, gp, vec[V_BPROJ],
    )


def solution(mesh):
    in_specs = (
        P(("dp", "row"), "col", None),
        P("row", None, "col"),
        P(None, "col"),
        P("col", "row"),
        P(),
        P(),
        P(),
        P(),
        P(),
        P("row", "col"),
        P("col"),
        P("col", "row"),
        P(),
        P(("dp", "row")),
        P(("dp", "row"), "col", None),
    )
    out_specs = (
        P(("dp", "row"), "col", None),
        P(("dp", "row"), "col", None),
        P(("dp", "row")),
        P("row", None, "col"),
        P(None, "col"),
        P("col", "row"),
        P(),
        P(),
        P(),
        P(),
        P(),
        P("row", "col"),
        P("col"),
        P("col", "row"),
        P(),
    )
    return jax.shard_map(shards, mesh=mesh, in_specs=in_specs, out_specs=out_specs, check_vma=False)
```

profile of v0, /device:TPU:0, one launch (start us, length us, event | category | flops | bytes accessed | tf_op | source)
XLA Modules:
  0.0 235.9 jit_solution(16864379277685234133)
XLA Ops:
  0.6 0.0 copy-start
  0.7 0.9 select_bitcast_fusion
  1.6 0.7 broadcast_in_dim.6
  2.3 0.7 convert_element_type.27
  2.9 0.1 pad.4.clone
  3.0 0.1 pad.5.clone
  3.1 0.7 maximum_maximum_fusion.misc_in
  3.8 2.4 %convert_element_type.25.x_in = bf16[2,256,768]{2,1,0:T(8,128)(2,1)} convert(f32[2,256,768]{2,1,0:T(8,128)} %param.15) | non-fusion elementwise | flops 393216 | bytes 2359296 | tf_op jit(solution)/shard_map/convert_element_type | solution.py:859
  6.1 0.0 copy-done
  6.1 0.0 copy-start.6
  6.1 0.0 copy-start.7
  6.1 0.0 copy-start.8
  6.1 0.0 copy-start.9
  6.2 0.0 copy-start.10
  6.2 0.0 copy-start.11
  6.2 1.0 convert_element_type.26.cot_in
  7.1 0.0 copy-done.6
  7.1 0.0 copy-done.7
  7.2 0.0 copy-done.8
  7.2 0.0 copy-done.9
  7.2 0.0 copy-done.10
  7.2 0.0 copy-done.11
  7.2 0.7 stack.29.vec_in
  7.9 216.7 %layer.1 = (bf16[2,256,768]{2,1,0:T(8,128)(2,1)}, bf16[2,256,768]{2,1,0:T(8,128)(2,1)}, bf16[3,192,384]{2,1,0:T(8,128)(2,1)}, bf16[192,384]{1,0:T(8,128)(2,1)}, ...) custom-call(bf16[2,256,768]{2,1,0:T(8,128)(2,1)} %convert_element_type.25.x_in, ...), custom_call_target="tpu_custom_call" | custom-call | tf_op jit(solution)/shard_map/layer/pallas_call | solution.py:781
  224.6 0.0 copy-start.1
  224.6 1.7 slice_reduce_fusion
  226.4 0.7 constant_dynamic-slice_fusion
  227.0 1.3 dynamic-slice_reduce_fusion.2
  228.3 2.4 %convert_element_type.28 = f32[2,256,768]{2,1,0:T(8,128)} convert(bf16[2,256,768]{2,1,0:T(8,128)(2,1)} %get-tuple-element.23) | non-fusion elementwise | flops 393216 | bytes 2359296 | tf_op jit(solution)/shard_map/convert_element_type | solution.py:861
  230.7 0.0 copy-start.3
  230.7 0.0 copy-done.1
  230.7 0.0 copy-start.2
  230.7 1.3 convert_element_type.29
  232.0 0.0 copy-done.3
  232.0 0.0 copy-start.4
  232.0 1.1 convert_element_type.31
  233.1 0.0 copy-start.5
  233.1 0.0 copy-done.2
  233.1 1.1 convert_element_type.32
  234.1 0.0 copy-done.4
  234.2 1.0 convert_bitcast_fusion
  235.1 0.0 copy-done.5
  235.1 0.7 convert_element_type.30
  (9 shorter events, 0.0 us)
Async XLA Ops:
  0.6 5.5 %copy-start = (f32[2,256,768]{2,1,0:T(8,128)S(1)}, f32[2,256,768]{2,1,0:T(8,128)}, u32[]{:S(2)}) copy-start(f32[2,256,768]{2,1,0:T(8,128)} %param.29) | copy-start | bytes 4718596
  6.1 1.0 copy-start.6
  6.1 1.0 copy-start.7
  6.1 1.0 copy-start.8
  6.1 1.0 copy-start.9
  6.2 1.1 copy-start.10
  6.2 1.1 copy-start.11
  224.6 6.1 %copy-start.1 = (bf16[2,256,768]{2,1,0:T(8,128)(2,1)S(1)}, bf16[2,256,768]{2,1,0:T(8,128)(2,1)}, u32[]{:S(2)}) copy-start(bf16[2,256,768]{2,1,0:T(8,128)(2,1)} %get-tuple-element.24) | copy-start | bytes 2359300
  230.7 1.3 copy-start.3
  230.7 2.4 copy-start.2
  232.0 2.2 copy-start.4
  233.1 2.1 copy-start.5
where the time goes:
time: 237 us; the launch traced here: 236 us
  Pallas kernels  217 us (92%)
  other arithmetic  13.1 us (6%)
  local copies, waits for them, and re-layouts  5.26 us (2%)
    pallas_call x1, Pallas kernels, shards(): pl.pallas_call(kernel, name='layer', out_shape=(jax.ShapeDtypeStruct((E,...  217 us
    convert_element_type x5, other arithmetic, shards(): lo, gi, gq, go, gf, gp = (v.astype(F32) for v in (lo, gi, gq, go, gf, gp))  6.55 us

commit v1 on v0

--- a/solution.py
+++ b/solution.py
@@ -45,12 +45,12 @@
 
 
 def kernel(
-    x_in, cot_in, wq_in, wo_in, wf_in, wp_in, misc_in, vec_in,
-    lo_out, gi_out, gq_out, go_out, gf_out, gp_out, vec_out, norm_out,
-    XR, H, A1, WQ, WO, WF, WP, MISC, QKV, CTX, LSE, KB, ACC,
+    x_in, cot_in, wq_in, wo_in, wf_in, wp_in, bfc_in, bqv_in, len_in, b_out, ln1_g, ln1_b, ln2_g, ln2_b, b_proj,
+    lo_out, gi_out, gq_out, go_out, gf_out, gp_out, vec_out,
+    XS, XH, CS, misc_in, XR, H, A1, WQ, WO, WF, WP, MISC, QKV, CTX, LSE, KB, ACC,
     PS, PR, A2, M, SL, GF, GA, GCTX, GQKV, DK, DV, LO, GI,
     V8, SQ, VF, VK, VP, VZ,
-    GWQ, GWO, GWF, GWP, RQ, RO, RF, RF2, RP, SQW, SOW, SFW, SFW2, SPW, ZQ, ZO, ZF, ZF2, ZP, EQ, EO, EF, EF2, EP,
+    GWQ, GWO, GWF, GWP, RQ, RO, RF, RF2, RP, SQW, SOW, SFW, SFW2, SPW, BQ, BO, BF1, BF2, BP, UQ, UO, UF, UF2, UP, ZQ, ZO, ZF, ZF2, ZP, EQ, EO, EF, EF2, EP,
     ss, rs,
 ):
     d, row, z = lax.axis_index("dp"), lax.axis_index("row"), lax.axis_index("col")
@@ -97,7 +97,12 @@
 
         def make():
             return pltpu.make_async_remote_copy(
-                src(), dst(), ss.at[sem], rs.at[rsem], device_id=dev, device_id_type=MESH
+                src(),
+                dst(),
+                ss.at[sem],
+                rs.at[rsem() if callable(rsem) else rsem],
+                device_id=dev() if callable(dev) else dev,
+                device_id_type=MESH,
             )
 
         when(cond, lambda: make().start())
@@ -139,9 +144,10 @@
         arrive(lambda: dst(i), base + i, jnp.logical_not(mine))
         arrive_local(lambda: dst(i), base + i, mine)
 
-    away = [2 * k + cs != z for cs in range(2)]
-    near_mate = [[(2 * k + cs == z) & (k != r) for r in range(2)] for cs in range(2)]
-    near_self = [[(2 * k + cs == z) & (k == r) for r in range(2)] for cs in range(2)]
+    far = lax.rem(k + zk, 2)
+    target = z ^ (2 * far)
+    is_near, is_far = far == 0, far == 1
+    zo = 1 - zs
 
     class Weight:
         def __init__(self, src, src_quarter, piece, full, slab):
@@ -149,34 +155,45 @@
             self.zsem, self.xsem = new_recv(4), new_recv(8)
 
         def push(self):
-            sem = self.zsem + zs * 2 + k
-            for j in (1, 2, 3):
-                send(self.src_quarter, lambda: self.piece(zs, k, dq), sem, at(d, zk, z ^ j))
-            send(self.src, lambda: self.full(zs, k), sem, mate, zk != k)
-            local(self.src, lambda: self.full(zs, k), sem, zk == k)
+            sem = lambda: self.zsem + zs * 2 + k
+            for j in (2, 1):
+                send(self.src_quarter, lambda: self.piece(zs, k, dq), sem, lambda j=j: at(d, zk, z ^ j))
+            send(self.src, lambda: self.full(zs, k), sem, mate, is_far)
+            local(self.src, lambda: self.full(zs, k), self.zsem + zs * 2 + k, is_near)
+
+        def spread(self, cs, cond):
+            mine = lambda: self.slab(cs, dq)
+            for j in (1, 2):
+                send(mine, mine, lambda j=j: self.xsem + cs * 4 + j - 1, quad[j - 1], cond)
+
+        def hop(self):
+            for r in range(2):
+                arrive(lambda: self.piece(zo, r, dq), self.zsem + zo * 2 + r, is_near)
+                arrive(lambda: self.piece(zs, r, dq), self.zsem + zs * 2 + r, is_far)
+                mine = lambda r=r: self.piece(zs, r, dq)
+                send(mine, mine, lambda r=r: self.zsem + zs * 2 + r, lambda: at(d, k, z ^ 1), is_far)
+            self.spread(zo, is_near)
+            self.spread(zs, is_far)
 
         def forward(self):
-            for cs in range(2):
-                for r in range(2):
-                    sem = self.zsem + cs * 2 + r
-                    arrive(lambda: self.piece(cs, r, dq), sem, away[cs])
-                    arrive(lambda: self.full(cs, r), sem, near_mate[cs][r])
-                    arrive_local(lambda: self.full(cs, r), sem, near_self[cs][r])
-                mine = lambda cs=cs: self.slab(cs, dq)
+            for r in range(2):
+                arrive(lambda: self.piece(zo, r, dq), self.zsem + zo * 2 + r, is_far)
+            self.spread(zo, is_far)
+
+        def relay(self):
+            for cs, cond in ((zs, is_far), (zo, True)):
                 for j in (1, 2):
-                    send(mine, mine, self.xsem + cs * 4 + j - 1, quad[j - 1], away[cs])
-
-        def relay(self):
-            for cs in range(2):
+                    arrive(lambda: self.slab(cs, dq ^ j), self.xsem + cs * 4 + j - 1, cond)
+                    half = lambda cs=cs, j=j: self.piece(cs, j - 1, dq ^ j)
+                    send(half, half, lambda cs=cs, j=j: self.xsem + cs * 4 + 1 + j, quad[2 - j], cond)
+
+        def ready(self):
+            for r in range(2):
+                arrive(lambda: self.full(zs, r), self.zsem + zs * 2 + r, is_near & (k != r))
+                arrive_local(lambda: self.full(zs, r), self.zsem + zs * 2 + r, is_near & (k == r))
+            for cs, cond in ((zs, is_far), (zo, True)):
                 for j in (1, 2):
-                    arrive(lambda: self.slab(cs, dq ^ j), self.xsem + cs * 4 + j - 1, away[cs])
-                    half = lambda cs=cs, j=j: self.piece(cs, j - 1, dq ^ j)
-                    send(half, half, self.xsem + cs * 4 + 1 + j, quad[2 - j], away[cs])
-
-        def ready(self):
-            for cs in range(2):
-                for j in (1, 2):
-                    arrive(lambda: self.piece(cs, j - 1, dq ^ 3), self.xsem + cs * 4 + 1 + j, away[cs])
+                    arrive(lambda: self.piece(cs, j - 1, dq ^ 3), self.xsem + cs * 4 + 1 + j, cond)
 
     q48, o48, f96, p192 = QR // QUAD, OR_ // QUAD, FR // QUAD, PR_ // QUAD
 
@@ -222,30 +239,65 @@
     w_fc, w_fc2 = fc_part(0, first), fc_part(first, FC - first)
     w_proj, w_proj2 = proj_part(0, first), proj_part(first, FC - first)
 
+    stage = new_recv(2)
+    pltpu.make_async_copy(x_in, H, rs.at[stage]).start()
+    pltpu.make_async_copy(cot_in, ACC, rs.at[stage + 1]).start()
+    bq, bv = bqv_in[0:1, :], bqv_in[1:2, :]
+    gap = jnp.zeros_like(bq)
+    misc_in[...] = jnp.concatenate(
+        [
+            bfc_in[...].reshape(1, D),
+            jnp.where(zs == 0, jnp.concatenate([bq, gap, bv, gap], axis=1), jnp.concatenate([gap, bq, gap, bv], axis=1)),
+            jnp.full((1, D), len_in[0].astype(F32)),
+            jnp.full((1, D), len_in[1].astype(F32)),
+            jnp.zeros((4, D), F32),
+        ],
+        axis=0,
+    )
     misc_sem = new_recv(8)
     for dev in line:
         send(lambda: misc_in, lambda: MISC.at[k, z], misc_sem + k * 4 + z, dev)
     local(lambda: misc_in, lambda: MISC.at[k, z], misc_sem + k * 4 + z)
     w_qkv.push()
-    x_sem = line_send(lambda i: x_in.at[i], lambda i: XR.at[i])
+    pltpu.make_async_copy(x_in, H, rs.at[stage]).wait()
+    XS[...] = H[...].astype(BF)
+    half_rows = T // 2
+    xh_sem, x_sem = new_recv(1), new_recv(4)
+    part_of = lambda core: pl.ds(mo(core * half_rows, 16), half_rows)
+    send(lambda: XS.at[:, part_of(1 - k)], lambda: XH, xh_sem, mate)
+    for i in range(2):
+        mine = is_near & (zs == i)
+        src, dst = lambda i=i: XS.at[i, part_of(k)], lambda: XR.at[zs, part_of(k)]
+        send(src, dst, x_sem + zs * 2 + k, at(d, zk, 2 * k + i), jnp.logical_not(mine))
+        local(src, dst, x_sem + zs * 2 + k, mine)
+    pltpu.make_async_copy(cot_in, ACC, rs.at[stage + 1]).wait()
+    CS[...] = ACC[...].astype(BF)
 
     V8[...] = jnp.zeros_like(V8)
     SQ[...] = jnp.zeros_like(SQ)
 
-    vec = lambda i: vec_in[i : i + 1, :]
-    b_out, ln1_g, ln1_b, ln2_g, ln2_b, b_proj = (vec(i) for i in range(6))
-
+    b_out, ln1_g, ln1_b, ln2_g, ln2_b, b_proj = (
+        v[...].reshape(1, D) for v in (b_out, ln1_g, ln1_b, ln2_g, ln2_b, b_proj)
+    )
+
+    w_qkv.hop()
+    arrive(lambda: XH, xh_sem)
+    for i in range(2):
+        send(lambda i=i: XH.at[i], dst, x_sem + zs * 2 + k, at(d, zk, 2 * (1 - k) + i))
     w_qkv.forward()
     w_qkv.relay()
 
-    RB = 32
+    RB = 128
     a1_sem = new_recv(2)
 
     def rows_of(base, i, n):
         return pl.ds(mo(base + i * n, 16), n)
 
     for s in range(2):
-        line_wait(lambda i: XR.at[i], x_sem, s)
+        for core in range(2):
+            here = is_near & (zs == s) & (k == core)
+            arrive(lambda: XR.at[s, part_of(core)], x_sem + s * 2 + core, jnp.logical_not(here))
+            arrive_local(lambda: XR.at[s, part_of(core)], x_sem + s * 2 + core, here)
 
         def first_norm(i, c):
             scaled, _ = norm_stats(XR[s, rows_of(0, i, RB), :].astype(F32))
@@ -267,21 +319,19 @@
 
     w_qkv.ready()
 
-    def project(i, c):
-        rows = rows_of(0, lax.rem(2 * k + i, 4), T)
+    def project(base):
+        rows = pl.ds(mo(base, 16), 2 * T)
         a = A1[rows, :]
         QKV[0, rows, :] = ((dot_t(a, WQ[0]) + bias_q).astype(BF).astype(F32) * (HEAD_DIM**-0.5)).astype(BF)
         QKV[1, rows, :] = dot_t(a, WQ[1]).astype(BF)
         QKV[2, rows, :] = (dot_t(a, WQ[2]) + bias_v).astype(BF)
-        return c
-
-    lax.fori_loop(0, 2, project, 0)
+
+    project(own)
     for s in range(2):
         arrive(lambda: A1.at[pl.ds(mo(other + s * T, 16), T), :], a1_sem + s)
-    for w in (w_out, w_fc, w_fc2, w_proj, w_proj2):
-        w.push()
-    cot_sem = line_send(lambda i: cot_in.at[i], lambda i: GF.at[pl.ds(mo(z * T, 16), T), :])
-    lax.fori_loop(2, 4, project, 0)
+    w_out.push()
+    w_fc.push()
+    project(other)
 
     key_place = lax.broadcasted_iota(jnp.int32, (L, 128), 0).astype(F32)
     KB[...] = jnp.where(key_place < length, 0.0, MASKED)
@@ -305,11 +355,32 @@
             return last
         return jnp.concatenate([s[: kv - QB], last], axis=0)
 
-    def attend(p):
+    def send_cot():
+        return line_send(lambda i: CS.at[i], lambda i: GF.at[pl.ds(mo(z * T, 16), T), :])
+
+    between = {
+        (0, 3): (w_out.hop, w_fc2.push),
+        (1, 0): (w_fc.hop,),
+        (1, 2): (w_out.forward, w_proj.push),
+        (1, 3): (w_fc.forward, w_fc2.hop),
+        (2, 0): (w_out.relay, w_proj2.push),
+        (2, 2): (w_fc.relay, w_proj.hop),
+        (2, 3): (w_fc2.forward,),
+    }
+
+    def attend(p, c):
         lanes = pl.ds(mo(p * 128, 128), 128)
         kp, vp = QKV[1, :, lanes], QKV[2, :, lanes]
         vt = vp.T
         for qb in range(NQ):
+            for (step, at_qb), work in between.items():
+                if at_qb == qb:
+
+                    @pl.when(p == step)
+                    def _():
+                        for do in work:
+                            do()
+
             kv = (qb + 1) * QB
             qp = QKV[0, qb * QB : kv, lanes]
             parts = []
@@ -321,35 +392,17 @@
                 LSE[pl.ds(2 * p + h, 1), qb * QB : kv] = top + jnp.log(total)
                 parts.append(dot(vt[:, :kv], e.astype(BF)) / total)
             CTX[qb * QB : kv, lanes] = jnp.where(low_row, parts[0], parts[1]).T.astype(BF)
-
-    def attend_step(p, c):
-        @pl.when(p == 1)
-        def _():
-            w_out.forward()
-            w_fc.forward()
-
-        @pl.when(p == 2)
-        def _():
-            w_out.relay()
-            w_fc.relay()
-
-        attend(p)
         return c
 
-    lax.fori_loop(0, HC // 128, attend_step, 0)
-    w_fc2.forward()
-
-    def split_sum(n, product, sums=None):
+    lax.fori_loop(0, HC // 128, attend, 0)
+    w_proj2.hop()
+
+    def split_sum(n, product):
         base = new_recv(2)
+        PS[n] = product(pl.ds(mo(other, 16), 2 * T)).astype(BF).reshape(2, T, D)
         for s in range(2):
-            PS[n, s] = product(pl.ds(mo(other + s * T, 16), T)).astype(BF)
             send(lambda s=s: PS.at[n, s], lambda s=s: PR.at[n, s], base + s, mate)
-
-        def keep(s, c):
-            ACC[s] = product(pl.ds(mo(own + s * T, 16), T))
-            return c
-
-        lax.fori_loop(0, 2, keep, 0)
+        ACC[...] = product(pl.ds(mo(own, 16), 2 * T)).reshape(2, T, D)
         return base
 
     def split_wait(n, base, s):
@@ -357,8 +410,8 @@
 
     w_out.ready()
     ex = split_sum(0, lambda rows: dot(CTX[rows, :], WO[...]))
-    w_fc2.relay()
     w_proj.forward()
+    cot_sem = send_cot()
     a2_sem = new_recv(2)
     for s in range(2):
         split_wait(0, ex, s)
@@ -377,10 +430,11 @@
 
     VF[...] = jnp.concatenate([MISC[0, 2 * k, 0:1, :], MISC[0, 2 * k + 1, 0:1, :]], axis=1)
 
-    def hidden(start, width):
+    def hidden(base, start, width):
+        rows = pl.ds(mo(base, 16), 2 * T)
+
         def body(i, c):
-            rows = rows_of(0, lax.rem(2 * k + i // 2, 4), T)
-            cs = pl.ds(mo(lax.rem(i, 2) * FC + start, 128), width)
+            cs = pl.ds(mo(i * FC + start, 128), width)
             u = dot(A2[rows, :], WF[:, :, cs].reshape(D, width)) + VF[:, cs]
             t = jnp.tanh(GELU_C * (u + GELU_A * u * u * u))
             M[rows, cs] = (0.5 * u * (1.0 + t)).astype(BF)
@@ -389,18 +443,20 @@
             ).astype(BF)
             return c
 
-        return body
+        lax.fori_loop(0, 2, body, 0)
 
     w_fc.ready()
-    lax.fori_loop(0, 4, hidden(0, first), 0)
+    hidden(own, 0, first)
+    w_fc2.relay()
     for s in range(2):
         arrive(lambda: A2.at[pl.ds(mo(other + s * T, 16), T), :], a2_sem + s)
-    lax.fori_loop(4, 8, hidden(0, first), 0)
+    hidden(other, 0, first)
     w_proj2.forward()
     w_proj.relay()
     w_fc2.ready()
-    lax.fori_loop(0, 8, hidden(first, FC - first), 0)
+    hidden(own, first, FC - first)
     w_proj2.relay()
+    hidden(other, first, FC - first)
     w_proj.ready()
     w_proj2.ready()
     ex = split_sum(1, lambda rows: dot(M[rows, :], WP[...]))
@@ -435,11 +491,12 @@
     for s in range(2):
         arrive(lambda: GF.at[pl.ds(mo(other + s * T, 16), T), :], gf_sem + s)
 
+
     class Part:
-        def __init__(self, quarter, R, S, Z, E, pieces, place):
-            self.quarter, self.R, self.S, self.Z, self.E = quarter, R, S, Z, E
-            self.pieces, self.place = pieces, place
-            self.raw, self.zsem, self.end = new_recv(3), new_recv(4), new_recv(4)
+        def __init__(self, quarter, R, S, B, U, Z, E, slab, piece, place):
+            self.quarter, self.R, self.S, self.B, self.U, self.Z, self.E = quarter, R, S, B, U, Z, E
+            self.slab, self.piece, self.place = slab, piece, place
+            self.raw, self.pair, self.zsem, self.end = new_recv(3), new_recv(1), new_recv(2), new_recv(4)
 
         def spread(self):
             for j in (1, 2, 3):
@@ -462,22 +519,22 @@
                 return c
 
             lax.fori_loop(0, 2 * steps, add, 0)
-            for cs in range(2):
-                for r in range(2):
-                    mine = (r == k) & (2 * k + cs == z)
-                    piece = lambda cs=cs, r=r: self.pieces(cs, r)
-                    send(piece, lambda: self.Z.at[z], self.zsem + z, at(d, r, 2 * k + cs), jnp.logical_not(mine))
-                    local(piece, lambda: self.Z.at[z], self.zsem + z, mine)
+            send(lambda: self.slab(1 - zs), lambda: self.B, self.pair, at(d, k, z ^ 1))
+
+        def middle(self):
+            arrive(lambda: self.B, self.pair)
+            self.U[...] = (self.slab(zs)[...].astype(F32) + self.B[...].astype(F32)).astype(BF)
+            for r in range(2):
+                mine = (far == 0) & (r == k)
+                piece = lambda r=r: self.piece(r)
+                send(piece, lambda: self.Z.at[far], self.zsem + far, at(d, r, target), jnp.logical_not(mine))
+                local(piece, lambda: self.Z.at[far], self.zsem + far, mine)
 
         def finish(self):
-            for c in range(4):
-                here = (zk == k) & (z == c)
-                arrive(lambda: self.Z.at[c], self.zsem + c, jnp.logical_not(here))
-                arrive_local(lambda: self.Z.at[c], self.zsem + c, here)
-            Z = self.Z
-            self.E[...] = (
-                Z[0].astype(F32) + Z[1].astype(F32) + Z[2].astype(F32) + Z[3].astype(F32)
-            ).astype(BF)
+            arrive(lambda: self.Z.at[0], self.zsem, is_far)
+            arrive_local(lambda: self.Z.at[0], self.zsem, is_near)
+            arrive(lambda: self.Z.at[1], self.zsem + 1)
+            self.E[...] = (self.Z[0].astype(F32) + self.Z[1].astype(F32)).astype(BF)
             for j in (1, 2, 3):
                 send(lambda: self.E, lambda: self.place(dq), self.end + j, quad[j - 1])
             local(lambda: self.E, lambda: self.place(dq), self.end)
@@ -488,50 +545,55 @@
                 arrive(lambda: self.place(dq ^ j), self.end + j)
 
     g_proj = Part(
-        lambda q: GWP.at[:, pl.ds(mo(q * p192, 16), p192), :], RP, SPW, ZP, EP,
-        lambda cs, r: SPW.at[cs, :, cols(r)],
+        lambda q: GWP.at[:, pl.ds(mo(q * p192, 16), p192), :], RP, SPW, BP, UP, ZP, EP,
+        lambda cs: SPW.at[cs],
+        lambda r: UP.at[:, cols(r)],
         lambda q: gp_out.at[pl.ds(mo(q * p192, 16), p192), :],
     )
     g_out = Part(
-        lambda q: GWO.at[:, pl.ds(mo(q * o48, 16), o48), :], RO, SOW, ZO, EO,
-        lambda cs, r: SOW.at[cs, :, cols(r)],
+        lambda q: GWO.at[:, pl.ds(mo(q * o48, 16), o48), :], RO, SOW, BO, UO, ZO, EO,
+        lambda cs: SOW.at[cs],
+        lambda r: UO.at[:, cols(r)],
         lambda q: go_out.at[pl.ds(mo(q * o48, 16), o48), :],
     )
 
-    def fc_grad(R, S, Z, E, start, n):
+    def fc_grad(R, S, B, U, Z, E, start, n):
         return Part(
-            lambda q: GWF.at[:, pl.ds(mo(start + q * n, 16), n), :], R, S, Z, E,
-            lambda cs, r: S.at[r, :, pl.ds(mo(cs * FC, 128), FC)],
+            lambda q: GWF.at[:, pl.ds(mo(start + q * n, 16), n), :], R, S, B, U, Z, E,
+            lambda cs: S.at[:, :, pl.ds(mo(cs * FC, 128), FC)],
+            lambda r: U.at[r],
             lambda q: gf_out.at[pl.ds(mo(start + q * n, 16), n), :],
         )
 
-    g_fc = fc_grad(RF, SFW, ZF, EF, 0, 128 // QUAD)
-    g_fc2 = fc_grad(RF2, SFW2, ZF2, EF2, 128, (FR - 128) // QUAD)
+    g_fc = fc_grad(RF, SFW, BF1, UF, ZF, EF, 0, 128 // QUAD)
+    g_fc2 = fc_grad(RF2, SFW2, BF2, UF2, ZF2, EF2, 128, (FR - 128) // QUAD)
 
     def qkv_grad(i):
         return Part(
-            lambda q: GWQ.at[i, :, pl.ds(mo(q * q48, 16), q48), :], RQ.at[i], SQW.at[i], ZQ.at[i], EQ.at[i],
-            lambda cs, r: SQW.at[i, cs, :, cols(r)],
+            lambda q: GWQ.at[i, :, pl.ds(mo(q * q48, 16), q48), :],
+            RQ.at[i], SQW.at[i], BQ.at[i], UQ.at[i], ZQ.at[i], EQ.at[i],
+            lambda cs: SQW.at[i, cs],
+            lambda r: UQ.at[i, :, cols(r)],
             lambda q: gq_out.at[i, pl.ds(mo(q * q48, 16), q48), :],
         )
 
     g_qkv = [qkv_grad(i) for i in range(3)]
 
     def grad_proj(i, c):
-        cs = pl.ds(mo(i * 256, 128), 256)
+        cs = pl.ds(mo(i * (FC // 2), 128), FC // 2)
         g = t_dot(M[:, cs], GF[...])
         SQ[...] += fold8(g * g)
-        GWP[i // 3, pl.ds(mo(lax.rem(i, 3) * 256, 16), 256), :] = g.astype(BF)
+        GWP[i // 2, pl.ds(mo(lax.rem(i, 2) * (FC // 2), 16), FC // 2), :] = g.astype(BF)
         return c
 
-    lax.fori_loop(0, FH // 256, grad_proj, 0)
+    lax.fori_loop(0, 4, grad_proj, 0)
     g_proj.spread()
 
     NB = 512
     NN = FH // NB
 
     def grad_hidden(i, c):
-        rows = rows_of(0, i // NN, T)
+        rows = pl.ds(mo(i // NN * 2 * T, 16), 2 * T)
         cs = pl.ds(mo(lax.rem(i, NN) * NB, 128), NB)
         g = dot_t(GF[rows, :], WP[cs, :]) * SL[rows, cs].astype(F32)
         low = g.astype(BF)
@@ -539,7 +601,7 @@
         VF[:, cs] = jnp.where(i < NN, 0.0, VF[:, cs]) + jnp.sum(low.astype(F32), axis=0, keepdims=True)
         return c
 
-    lax.fori_loop(0, 4 * NN, grad_hidden, 0)
+    lax.fori_loop(0, 2 * NN, grad_hidden, 0)
     ex = split_sum(2, lambda rows: dot_t(SL[rows, :], WF[...].reshape(D, FH)))
 
     ga_sem = new_recv(2)
@@ -570,37 +632,21 @@
     for s in range(2):
         arrive(lambda: GA.at[pl.ds(mo(other + s * T, 16), T), :], ga_sem + s)
 
-    def grad_context(i, c):
-        rows = rows_of(0, i, T)
-        GCTX[rows, :] = dot_t(GA[rows, :], WO[...]).astype(BF)
-        return c
-
-    lax.fori_loop(0, 4, grad_context, 0)
+    GCTX[...] = dot_t(GA[...], WO[...]).astype(BF)
     half = HC // 2
-    for cs in range(HC // 128):
-        g = t_dot(CTX[:, cs * 128 : (cs + 1) * 128], GA[...])
-        SQ[...] += fold8(g * g)
-        low = g.astype(BF)
-        lo_row = cs * 128
-        if lo_row + 128 <= half:
-            GWO[0, lo_row : lo_row + 128, :] = low
-        elif lo_row >= half:
-            GWO[1, lo_row - half : lo_row - half + 128, :] = low
-        else:
-            GWO[0, lo_row:half, :] = low[: half - lo_row]
-            GWO[1, : lo_row + 128 - half, :] = low[half - lo_row :]
+    g = t_dot(CTX[...], GA[...])
+    SQ[...] += fold8(g * g)
+    GWO[0] = g[:half].astype(BF)
+    GWO[1] = g[half:].astype(BF)
     g_out.spread()
 
-    def grad_fc(i, c):
-        block = lax.rem(i, 2) * 3 + i // 2
-        cs = pl.ds(mo(block * 128, 128), 128)
-        g = t_dot(A2[:, cs], SL[...])
+    def grad_fc(start, n):
+        g = t_dot(jnp.concatenate([A2[:, start : start + n], A2[:, FR + start : FR + start + n]], axis=1), SL[...])
         q = fold8(g * g)
         SQ[...] += q[:, :D] + q[:, D:]
-        GWF[lax.rem(i, 2), pl.ds(mo(i // 2 * 128, 16), 128), :] = g.astype(BF)
-        return c
-
-    lax.fori_loop(0, 2, grad_fc, 0)
+        GWF[:, start : start + n, :] = g.astype(BF).reshape(2, n, FH)
+
+    grad_fc(0, 128)
     g_fc.spread()
 
     def attend_back(p):
@@ -639,7 +685,7 @@
         return dot(GQKV[0, rows, :], WQ[0]) + dot(GQKV[1, rows, :], WQ[1]) + dot(GQKV[2, rows, :], WQ[2])
 
     ex = split_sum(3, grad_norm_in)
-    lax.fori_loop(2, D // 128, grad_fc, 0)
+    grad_fc(128, FR - 128)
     for s in range(2):
         split_wait(3, ex, s)
 
@@ -710,16 +756,28 @@
     order = [g_proj, g_out, g_fc, g_fc2, *g_qkv]
     for i, part in enumerate(order):
         part.reduce()
+        if i >= 1:
+            order[i - 1].middle()
         if i >= 2:
             order[i - 2].finish()
+    order[-1].middle()
     for part in order[-2:]:
         part.finish()
 
     for j in (1, 2, 3):
         arrive(lambda: VZ.at[z ^ j], vz_sem + j - 1)
-    vec_out[...] = (VZ[0] + VZ[1] + VZ[2] + VZ[3])[0:12]
-    for c in range(4):
-        norm_out[c : c + 1, :] = VZ[c, V_NORM : V_NORM + 1, 0:128]
+    total = VZ[0] + VZ[1] + VZ[2] + VZ[3]
+    vec_out[0:6, :] = total[0:6]
+    V8[0, 0:6, :] = total[6:12]
+    vec_out[6:7, :] = V8[0, pl.ds(V_BFC - V_BQV + 3 * zk + zs, 1), :]
+    pair = V8[0, pl.ds(3 * zk, 1), :]
+    spare = jnp.zeros((1, D - QR), F32)
+    for i in range(2):
+        a, b = pair[:, i * HC : i * HC + QR], pair[:, i * HC + QR : (i + 1) * HC]
+        vec_out[7 + i : 8 + i, :] = jnp.concatenate([jnp.where(zs == 0, a, b), spare], axis=1)
+    vec_out[9:10, :] = VZ[2 * k, V_NORM : V_NORM + 1, :]
+    vec_out[10:11, :] = VZ[2 * k + 1, V_NORM : V_NORM + 1, :]
+    vec_out[11:12, :] = jnp.zeros((1, D), F32)
 
     for part in order:
         part.done()
@@ -754,23 +812,6 @@
     FQ = w_fc.shape[1]
     FH = FQ * n_col // 2
     DH = w_fc.shape[0]
-    c = lax.axis_index("col")
-
-    zero = jnp.zeros_like(b_qv)
-    even = lax.rem(c, 2) == 0
-    both = jnp.where(
-        even, jnp.concatenate([b_qv, zero], axis=1), jnp.concatenate([zero, b_qv], axis=1)
-    ).reshape(1, 2 * HC)
-    misc = jnp.concatenate(
-        [
-            b_fc[None, :],
-            both,
-            jnp.broadcast_to(lengths.astype(F32)[:, None], (E, D)),
-            jnp.zeros((4, D), F32),
-        ],
-        axis=0,
-    )
-    vecs = jnp.stack([b_out, ln1_g, ln1_b, ln2_g, ln2_b, b_proj, b_proj, b_proj])
     wq_t = jnp.transpose(w_qkv, (1, 2, 0))
     q48, o48, p192 = HQ // QUAD, HQ // QUAD, FQ // QUAD
     fa, fb = 128 // QUAD, (DH - 128) // QUAD
@@ -789,11 +830,14 @@
             jax.ShapeDtypeStruct((DH, FQ), BF),
             jax.ShapeDtypeStruct((FQ, DH), BF),
             jax.ShapeDtypeStruct((12, D), F32),
-            jax.ShapeDtypeStruct((8, 128), F32),
         ),
-        in_specs=[anyspec] * 7 + [vm],
-        out_specs=(anyspec,) * 6 + (vm, vm),
+        in_specs=[anyspec] * 6 + [vm, vm, pl.BlockSpec(memory_space=pltpu.SMEM)] + [vm] * 6,
+        out_specs=(anyspec,) * 6 + (vm,),
         scratch_shapes=[
+            V((2, T, D), BF),
+            V((2, T // 2, D), BF),
+            V((2, T, D), BF),
+            V((8, D), F32),
             V((2, T, D), BF),
             V((2, T, D), F32),
             V((L, D), BF),
@@ -840,11 +884,16 @@
             V((2, fa, FH), BF),
             V((2, fb, FH), BF),
             V((2, p192, D), BF),
-            V((3, 4, q48, DH), BF),
-            V((4, o48, DH), BF),
-            V((4, fa, FQ), BF),
-            V((4, fb, FQ), BF),
-            V((4, p192, DH), BF),
+            *[
+                V(shape, BF)
+                for _ in "BU"
+                for shape in ((3, q48, D), (o48, D), (2, fa, FQ), (2, fb, FQ), (p192, D))
+            ],
+            V((3, 2, q48, DH), BF),
+            V((2, o48, DH), BF),
+            V((2, fa, FQ), BF),
+            V((2, fb, FQ), BF),
+            V((2, p192, DH), BF),
             V((3, q48, DH), BF),
             V((o48, DH), BF),
             V((fa, FQ), BF),
@@ -856,8 +905,12 @@
         compiler_params=pltpu.CompilerParams(
             collective_id=0, has_side_effects=True, vmem_limit_bytes=63 * 2**20
         ),
-    )(layer_in.astype(BF), cotangent.astype(BF), wq_t, w_out, w_fc, w_proj, misc, vecs)
-    lo, gi, gq, go, gf, gp, vec, norms = outs
+    )(
+        layer_in, cotangent, wq_t, w_out, w_fc, w_proj, b_fc, b_qv, lengths,
+        b_out, ln1_g, ln1_b, ln2_g, ln2_b, b_proj,
+    )
+    lo, gi, gq, go, gf, gp, vec = outs
+    norms = vec[9:11, 0]
     lo, gi, gq, go, gf, gp = (v.astype(F32) for v in (lo, gi, gq, go, gf, gp))
     gq = jnp.transpose(gq, (2, 0, 1))
     if pairs > 1:
@@ -873,16 +926,10 @@
             return lax.dynamic_slice_in_dim(whole, r * part, part, axis)
 
         gq, go, gf, gp = share(gq, 0), share(go, 1), share(gf, 0), share(gp, 1)
-    sample_norms = lax.dynamic_slice_in_dim(norms[:, 0], 2 * core, 2, 0)
-    row = 6 + 3 * (c // 2)
-    part = lax.rem(c, 2)
-    bqv = lax.dynamic_slice(vec, (row, 0), (1, D)).reshape(2, HC)
-    grad_bqv = lax.dynamic_slice(bqv, (0, part * HQ), (2, HQ))
-    grad_bfc = lax.dynamic_slice(vec, (row + 1 + part, 0), (1, D))[0]
     return (
-        lo, gi, sample_norms, gq, grad_bqv, go,
+        lo, gi, norms, gq, vec[7:9, :HQ], go,
         vec[V_BOUT], vec[V_LN1G], vec[V_LN1B], vec[V_LN2G], vec[V_LN2B],
-        gf, grad_bfc, gp, vec[V_BPROJ],
+        gf, vec[6], gp, vec[V_BPROJ],
     )
 
 

time: 237 us -> 204 us (0.86)
  Pallas kernels: 217 us -> 191 us
  other arithmetic: 13.1 us -> 7.52 us
    pallas_call x1, Pallas kernels: 217 us -> 191 us  [shards(): pl.pallas_call(kernel, name='layer', out_shape=(jax.ShapeDtypeStruct((E,...]
    convert_element_type x3 -> x0, other arithmetic: 3.98 us -> none  [the longest x1 2.36 us: shards(): layer_in.astype(BF)]
    slice x0 -> x2, local copies, waits for them, and re-layouts: none -> 2.6 us  [the longest x1 1.3 us: shards(): norms = vec[9:11, 0]]
where the time goes in v1:
time: 204 us
  Pallas kernels  191 us (94%)
  other arithmetic  7.52 us (4%)
  local copies, waits for them, and re-layouts  4.29 us (2%)
    pallas_call x1, Pallas kernels, shards(): pl.pallas_call(kernel, name='layer', out_shape=(jax.ShapeDtypeStruct((E,...  191 us
    convert_element_type x5, other arithmetic, shards(): lo, gi, gq, go, gf, gp = (v.astype(F32) for v in (lo, gi, gq, go, gf, gp))  6.55 us

profile of v1, /device:TPU:0, one launch (start us, length us, event | category | flops | bytes accessed | tf_op | source)
XLA Modules:
  0.0 203.8 jit_solution(15611982868395611272)
XLA Ops:
  0.7 191.3 %layer.1 = (bf16[2,256,768]{2,1,0:T(8,128)(2,1)}, bf16[2,256,768]{2,1,0:T(8,128)(2,1)}, bf16[3,192,384]{2,1,0:T(8,128)(2,1)}, bf16[192,384]{1,0:T(8,128)(2,1)}, ...) custom-call(f32[2,256,768]{2,1,0:T(8,128)} %x_in.1, f32[2,256,768]{2,1,0:T(8,128)} %cot_in.1, ...), custom_call_target="tpu_custom_call" | custom-call | tf_op jit(solution)/shard_map/layer/pallas_call | solution.py:822
  192.0 0.0 copy-start
  192.0 1.7 slice_reduce_fusion
  193.6 1.3 slice.28
  194.9 1.3 slice_reduce_fusion.7
  196.2 2.4 %convert_element_type.16 = f32[2,256,768]{2,1,0:T(8,128)} convert(bf16[2,256,768]{2,1,0:T(8,128)(2,1)} %get-tuple-element.22) | non-fusion elementwise | flops 393216 | bytes 2359296 | tf_op jit(solution)/shard_map/convert_element_type | solution.py:914
  198.6 0.0 copy-start.2
  198.6 0.0 copy-done
  198.6 0.0 copy-start.1
  198.6 1.3 convert_element_type.17
  199.9 0.0 copy-done.2
  199.9 0.0 copy-start.3
  199.9 1.1 convert_element_type.19
  201.0 0.0 copy-start.4
  201.0 0.0 copy-done.1
  201.0 1.1 convert_element_type.20
  202.1 0.0 copy-done.3
  202.1 1.0 convert_bitcast_fusion
  203.0 0.0 copy-done.4
  203.0 0.7 convert_element_type.18
Async XLA Ops:
  192.0 6.7 %copy-start = (bf16[2,256,768]{2,1,0:T(8,128)(2,1)S(1)}, bf16[2,256,768]{2,1,0:T(8,128)(2,1)}, u32[]{:S(2)}) copy-start(bf16[2,256,768]{2,1,0:T(8,128)(2,1)} %get-tuple-element.23) | copy-start | bytes 2359300
  198.6 1.3 copy-start.2
  198.6 2.4 %copy-start.1 = (bf16[768,384]{1,0:T(8,128)(2,1)S(1)}, bf16[768,384]{1,0:T(8,128)(2,1)}, u32[]{:S(2)}) copy-start(bf16[768,384]{1,0:T(8,128)(2,1)} %get-tuple-element.28) | copy-start | bytes 1769476
  199.9 2.2 %copy-start.3 = (bf16[3,192,384]{2,1,0:T(8,128)(2,1)S(1)}, bf16[3,192,384]{2,1,0:T(8,128)(2,1)}, u32[]{:S(2)}) copy-start(bf16[3,192,384]{2,1,0:T(8,128)(2,1)} %get-tuple-element.25) | copy-start | bytes 1327108
  201.0 2.1 %copy-start.4 = (bf16[192,384]{1,0:T(8,128)(2,1)S(1)}, bf16[192,384]{1,0:T(8,128)(2,1)}, u32[]{:S(2)}) copy-start(bf16[192,384]{1,0:T(8,128)(2,1)} %get-tuple-element.26) | copy-start | bytes 442372

commit v2 on v1

--- a/solution.py
+++ b/solution.py
@@ -19,7 +19,7 @@
 F32 = jnp.float32
 
 V_BOUT, V_LN1G, V_LN1B, V_LN2G, V_LN2B, V_BPROJ, V_BQV, V_BFC, V_SQ = 0, 1, 2, 3, 4, 5, 6, 7, 9
-V_FACTOR, V_NORM = 12, 13
+V_NORM = 12
 
 
 def dot(a, b):
@@ -49,8 +49,8 @@
     lo_out, gi_out, gq_out, go_out, gf_out, gp_out, vec_out,
     XS, XH, CS, misc_in, XR, H, A1, WQ, WO, WF, WP, MISC, QKV, CTX, LSE, KB, ACC,
     PS, PR, A2, M, SL, GF, GA, GCTX, GQKV, DK, DV, LO, GI,
-    V8, SQ, VF, VK, VP, VZ,
-    GWQ, GWO, GWF, GWP, RQ, RO, RF, RF2, RP, SQW, SOW, SFW, SFW2, SPW, BQ, BO, BF1, BF2, BP, UQ, UO, UF, UF2, UP, ZQ, ZO, ZF, ZF2, ZP, EQ, EO, EF, EF2, EP,
+    V8, SQ, VF, VK, FAC, VP, VZ,
+    GWQ, GWO, GWF, GWF2, GWP, RP, XQ, XO, XF, XF2, OQ, OO, OF, OF2, YQ, YO, YF, YF2, SQW, SOW, SFW, SFW2, SPW, BQ, BO, BF1, BF2, BP, UQ, UO, UF, UF2, UP, ZQ, ZO, ZF, ZF2, ZP, EQ, EO, EF, EF2, EP,
     ss, rs,
 ):
     d, row, z = lax.axis_index("dp"), lax.axis_index("row"), lax.axis_index("col")
@@ -131,9 +131,9 @@
         pl.semaphore_signal(barrier, inc=1, device_id=dev, device_id_type=MESH)
     pl.semaphore_wait(barrier, len(quad) + len(line))
 
-    def line_send(src, dst):
-        base = new_recv(2)
-        for i in range(2):
+    def line_send(src, dst, parts=(0, 1), base=None):
+        base = new_recv(2) if base is None else base
+        for i in parts:
             mine = (zk == k) & (2 * k + i == z)
             send(lambda i=i: src(i), lambda: dst(zs), base + zs, at(d, zk, 2 * k + i), jnp.logical_not(mine))
             local(lambda i=i: src(i), lambda: dst(zs), base + zs, mine)
@@ -491,34 +491,19 @@
     for s in range(2):
         arrive(lambda: GF.at[pl.ds(mo(other + s * T, 16), T), :], gf_sem + s)
 
+    bit = (lax.rem(dq, 2), dq // 2)
+
+    def wide_factors(count, width):
+        return [jnp.concatenate([FAC[dq ^ j, 0:1, :]] * (width // 128), axis=1) for j in range(count)]
 
     class Part:
-        def __init__(self, quarter, R, S, B, U, Z, E, slab, piece, place):
-            self.quarter, self.R, self.S, self.B, self.U, self.Z, self.E = quarter, R, S, B, U, Z, E
+        def __init__(self, plane, S, B, U, Z, E, slab, piece, place):
+            self.S, self.B, self.U, self.Z, self.E = S, B, U, Z, E
             self.slab, self.piece, self.place = slab, piece, place
-            self.raw, self.pair, self.zsem, self.end = new_recv(3), new_recv(1), new_recv(2), new_recv(4)
-
-        def spread(self):
-            for j in (1, 2, 3):
-                send(lambda j=j: self.quarter(dq ^ j), lambda j=j: self.R.at[j - 1], self.raw + j - 1, quad[j - 1])
-
-        def reduce(self):
-            for j in (1, 2, 3):
-                arrive(lambda: self.R.at[j - 1], self.raw + j - 1)
-            G, (_, n, width) = self.quarter(dq), self.S.shape
-            wide = lambda f: f if width <= D else jnp.concatenate([f] * (width // D), axis=1)
-            factors = [wide(VP[dq ^ j, V_FACTOR : V_FACTOR + 1, :]) for j in range(QUAD)]
-            steps = n // 16
-
-            def add(i, c):
-                a, rows = i // steps, pl.ds(mo(lax.rem(i, steps) * 16, 16), 16)
-                v = G[a, rows, :].astype(F32) * factors[0]
-                for j in (1, 2, 3):
-                    v = v + self.R[j - 1, a, rows, :].astype(F32) * factors[j]
-                self.S[a, rows, :] = v.astype(BF)
-                return c
-
-            lax.fori_loop(0, 2 * steps, add, 0)
+            self.pair, self.zsem, self.end = new_recv(1), new_recv(2), new_recv(4)
+            self.setup(*plane)
+
+        def pass_on(self):
             send(lambda: self.slab(1 - zs), lambda: self.B, self.pair, at(d, k, z ^ 1))
 
         def middle(self):
@@ -544,34 +529,94 @@
             for j in (1, 2, 3):
                 arrive(lambda: self.place(dq ^ j), self.end + j)
 
-    g_proj = Part(
-        lambda q: GWP.at[:, pl.ds(mo(q * p192, 16), p192), :], RP, SPW, BP, UP, ZP, EP,
+    class DirectPart(Part):
+        def setup(self, G, R):
+            self.G, self.R, self.raw = G, R, new_recv(3)
+
+        def quarter(self, q):
+            return self.G.at[:, q // 2, lax.rem(q, 2)]
+
+        def spread(self):
+            for j in (1, 2, 3):
+                send(lambda j=j: self.quarter(dq ^ j), lambda j=j: self.R.at[j - 1], self.raw + j - 1, quad[j - 1])
+
+        def reduce(self):
+            for j in (1, 2, 3):
+                arrive(lambda: self.R.at[j - 1], self.raw + j - 1)
+            G, (_, n, width) = self.quarter(dq), self.S.shape
+            factors, steps = wide_factors(QUAD, width), n // 16
+
+            def add(i, c):
+                a, rows = i // steps, pl.ds(mo(lax.rem(i, steps) * 16, 16), 16)
+                v = G[a, rows, :].astype(F32) * factors[0]
+                for j in (1, 2, 3):
+                    v = v + self.R[j - 1, a, rows, :].astype(F32) * factors[j]
+                self.S[a, rows, :] = v.astype(BF)
+                return c
+
+            lax.fori_loop(0, 2 * steps, add, 0)
+            self.pass_on()
+
+    class CrossPart(Part):
+        def setup(self, G, X, O, Y):
+            self.G, self.X, self.O, self.Y = G, X, O, Y
+            self.raw, self.cross = new_recv(2), new_recv(2)
+
+        def spread(self):
+            send(lambda: self.G.at[0, :, 1 - bit[0]], lambda: self.X.at[0], self.raw, quad[0])
+            send(lambda: self.G.at[1, 1 - bit[1]], lambda: self.X.at[1], self.raw + 1, quad[1])
+
+        def scale(self):
+            _, n, width = self.S.shape
+            factors = wide_factors(3, width)
+            for a in range(2):
+                arrive(lambda: self.X.at[a], self.raw + a)
+
+                def add(i, c, a=a):
+                    rows = pl.ds(mo(i * 16, 16), 16)
+                    for b, to in ((bit[1 - a], self.S), (1 - bit[1 - a], self.O)):
+                        mine = self.G[0, b, bit[0], rows, :] if a == 0 else self.G[1, bit[1], b, rows, :]
+                        v = mine.astype(F32) * factors[0] + self.X[a, b, rows, :].astype(F32) * factors[1 + a]
+                        to[a, rows, :] = v.astype(BF)
+                    return c
+
+                lax.fori_loop(0, n // 16, add, 0)
+                send(lambda a=a: self.O.at[a], lambda a=a: self.Y.at[a], self.cross + a, quad[1 - a])
+
+        def reduce(self):
+            for a in range(2):
+                arrive(lambda: self.Y.at[a], self.cross + a)
+            self.S[...] = (self.S[...].astype(F32) + self.Y[...].astype(F32)).astype(BF)
+            self.pass_on()
+
+    g_proj = DirectPart(
+        (GWP, RP), SPW, BP, UP, ZP, EP,
         lambda cs: SPW.at[cs],
         lambda r: UP.at[:, cols(r)],
         lambda q: gp_out.at[pl.ds(mo(q * p192, 16), p192), :],
     )
-    g_out = Part(
-        lambda q: GWO.at[:, pl.ds(mo(q * o48, 16), o48), :], RO, SOW, BO, UO, ZO, EO,
+    g_out = CrossPart(
+        (GWO, XO, OO, YO), SOW, BO, UO, ZO, EO,
         lambda cs: SOW.at[cs],
         lambda r: UO.at[:, cols(r)],
         lambda q: go_out.at[pl.ds(mo(q * o48, 16), o48), :],
     )
 
-    def fc_grad(R, S, B, U, Z, E, start, n):
-        return Part(
-            lambda q: GWF.at[:, pl.ds(mo(start + q * n, 16), n), :], R, S, B, U, Z, E,
+    def fc_grad(plane, S, B, U, Z, E, start, n):
+        return CrossPart(
+            plane, S, B, U, Z, E,
             lambda cs: S.at[:, :, pl.ds(mo(cs * FC, 128), FC)],
             lambda r: U.at[r],
             lambda q: gf_out.at[pl.ds(mo(start + q * n, 16), n), :],
         )
 
-    g_fc = fc_grad(RF, SFW, BF1, UF, ZF, EF, 0, 128 // QUAD)
-    g_fc2 = fc_grad(RF2, SFW2, BF2, UF2, ZF2, EF2, 128, (FR - 128) // QUAD)
+    g_fc = fc_grad((GWF, XF, OF, YF), SFW, BF1, UF, ZF, EF, 0, 128 // QUAD)
+    g_fc2 = fc_grad((GWF2, XF2, OF2, YF2), SFW2, BF2, UF2, ZF2, EF2, 128, (FR - 128) // QUAD)
 
     def qkv_grad(i):
-        return Part(
-            lambda q: GWQ.at[i, :, pl.ds(mo(q * q48, 16), q48), :],
-            RQ.at[i], SQW.at[i], BQ.at[i], UQ.at[i], ZQ.at[i], EQ.at[i],
+        return CrossPart(
+            [v.at[i] for v in (GWQ, XQ, OQ, YQ)],
+            *(v.at[i] for v in (SQW, BQ, UQ, ZQ, EQ)),
             lambda cs: SQW.at[i, cs],
             lambda r: UQ.at[i, :, cols(r)],
             lambda q: gq_out.at[i, pl.ds(mo(q * q48, 16), q48), :],
@@ -583,7 +628,7 @@
         cs = pl.ds(mo(i * (FC // 2), 128), FC // 2)
         g = t_dot(M[:, cs], GF[...])
         SQ[...] += fold8(g * g)
-        GWP[i // 2, pl.ds(mo(lax.rem(i, 2) * (FC // 2), 16), FC // 2), :] = g.astype(BF)
+        GWP[i // 2, lax.rem(i, 2)] = g.astype(BF).reshape(2, p192, D)
         return c
 
     lax.fori_loop(0, 4, grad_proj, 0)
@@ -633,20 +678,18 @@
         arrive(lambda: GA.at[pl.ds(mo(other + s * T, 16), T), :], ga_sem + s)
 
     GCTX[...] = dot_t(GA[...], WO[...]).astype(BF)
-    half = HC // 2
     g = t_dot(CTX[...], GA[...])
     SQ[...] += fold8(g * g)
-    GWO[0] = g[:half].astype(BF)
-    GWO[1] = g[half:].astype(BF)
+    GWO[...] = g.astype(BF).reshape(2, 2, 2, o48, D)
     g_out.spread()
 
-    def grad_fc(start, n):
+    def grad_fc(G, start, n):
         g = t_dot(jnp.concatenate([A2[:, start : start + n], A2[:, FR + start : FR + start + n]], axis=1), SL[...])
         q = fold8(g * g)
         SQ[...] += q[:, :D] + q[:, D:]
-        GWF[:, start : start + n, :] = g.astype(BF).reshape(2, n, FH)
-
-    grad_fc(0, 128)
+        G[...] = g.astype(BF).reshape(2, 2, 2, n // QUAD, FH)
+
+    grad_fc(GWF, 0, 128)
     g_fc.spread()
 
     def attend_back(p):
@@ -685,7 +728,8 @@
         return dot(GQKV[0, rows, :], WQ[0]) + dot(GQKV[1, rows, :], WQ[1]) + dot(GQKV[2, rows, :], WQ[2])
 
     ex = split_sum(3, grad_norm_in)
-    grad_fc(128, FR - 128)
+    grad_fc(GWF2, 128, FR - 128)
+    g_fc2.spread()
     for s in range(2):
         split_wait(3, ex, s)
 
@@ -706,14 +750,12 @@
 
         lax.fori_loop(0, T // RB, first_back, 0)
 
-    gi_sem = line_send(lambda i: GI.at[i], lambda i: gi_out.at[i])
+    gi_sem = line_send(lambda i: GI.at[i], lambda i: gi_out.at[i], (0,))
 
     def grad_qkv(i, c):
         g = t_dot(GQKV[i], A1[...])
         SQ[...] += fold8(g * g)
-        low = g.astype(BF)
-        GWQ[i, 0] = low[:half]
-        GWQ[i, 1] = low[half:]
+        GWQ[i] = g.astype(BF).reshape(2, 2, 2, q48, D)
         return c
 
     lax.fori_loop(0, 3, grad_qkv, 0)
@@ -734,34 +776,49 @@
     squares = jnp.sum(jnp.sum(pack * pack, axis=0, keepdims=True) + va[9:10] + vb[9:10], axis=1, keepdims=True)
     norm = jnp.sqrt(squares)
     factor = CLIP_BOUND / jnp.maximum(norm, CLIP_BOUND)
-    wide = lambda v: jnp.broadcast_to(v, (1, D))
-    VP[dq] = jnp.concatenate([pack, wide(factor), wide(norm), jnp.zeros((2, D), F32)], axis=0)
-    vp_sem = new_recv(3)
+    FAC[dq] = jnp.broadcast_to(factor, (8, 128))
+    fac_sem, vp_sem = new_recv(3), new_recv(3)
+    for j in (1, 2, 3):
+        send(lambda: FAC.at[dq], lambda: FAC.at[dq], fac_sem + j - 1, quad[j - 1])
+    VP[dq] = jnp.concatenate([pack, jnp.zeros((4, D), F32)], axis=0)
+    for part in g_qkv:
+        part.spread()
+
+    for j in (1, 2, 3):
+        arrive(lambda: FAC.at[dq ^ j], fac_sem + j - 1)
+
+    order = [g_proj, g_out, g_fc, g_fc2, *g_qkv]
+    g_proj.reduce()
+    for part in order[1:]:
+        part.scale()
     for j in (1, 2, 3):
         send(lambda: VP.at[dq], lambda: VP.at[dq], vp_sem + j - 1, quad[j - 1])
-    for part in (g_fc2, *g_qkv):
-        part.spread()
-
+    g_out.reduce()
+    g_fc.reduce()
+    g_proj.middle()
+    g_out.middle()
+    g_fc2.reduce()
+    g_fc.middle()
     for j in (1, 2, 3):
         arrive(lambda: VP.at[dq ^ j], vp_sem + j - 1)
-
     total = jnp.zeros((12, D), F32)
     for q in range(QUAD):
-        total = total + VP[q, 0:12, :] * VP[q, V_FACTOR : V_FACTOR + 1, :]
-    VZ[z] = jnp.concatenate([total, VP[dq, V_FACTOR:, :]], axis=0)
+        total = total + VP[q, 0:12, :] * FAC[q, 0:1, 0:1]
+    VZ[z] = jnp.concatenate([total, jnp.broadcast_to(norm, (4, D))], axis=0)
     vz_sem = new_recv(3)
     for j in (1, 2, 3):
         send(lambda: VZ.at[z], lambda: VZ.at[z], vz_sem + j - 1, at(d, k, z ^ j))
-
-    order = [g_proj, g_out, g_fc, g_fc2, *g_qkv]
-    for i, part in enumerate(order):
+    for part in g_qkv:
         part.reduce()
-        if i >= 1:
-            order[i - 1].middle()
-        if i >= 2:
-            order[i - 2].finish()
-    order[-1].middle()
-    for part in order[-2:]:
+    g_proj.finish()
+    g_fc2.middle()
+    g_out.finish()
+    g_fc.finish()
+    for part in g_qkv:
+        part.middle()
+    line_send(lambda i: GI.at[i], lambda i: gi_out.at[i], (1,), gi_sem)
+    g_fc2.finish()
+    for part in g_qkv:
         part.finish()
 
     for j in (1, 2, 3):
@@ -775,9 +832,11 @@
     for i in range(2):
         a, b = pair[:, i * HC : i * HC + QR], pair[:, i * HC + QR : (i + 1) * HC]
         vec_out[7 + i : 8 + i, :] = jnp.concatenate([jnp.where(zs == 0, a, b), spare], axis=1)
-    vec_out[9:10, :] = VZ[2 * k, V_NORM : V_NORM + 1, :]
-    vec_out[10:11, :] = VZ[2 * k + 1, V_NORM : V_NORM + 1, :]
-    vec_out[11:12, :] = jnp.zeros((1, D), F32)
+    first_place = lax.broadcasted_iota(jnp.int32, (1, D), 1) == 0
+    vec_out[9:10, :] = jnp.where(
+        first_place, VZ[2 * k, V_NORM : V_NORM + 1, :], VZ[2 * k + 1, V_NORM : V_NORM + 1, :]
+    )
+    vec_out[10:12, :] = jnp.zeros((2, D), F32)
 
     for part in order:
         part.done()
@@ -786,6 +845,35 @@
         line_wait(lambda i: gi_out.at[i], gi_sem, i)
     for cond, make in pending:
         when(cond, lambda: make().wait_send())
+
+
+def widen(*refs):
+    low, vec, wide, (b_out, ln1_g, ln1_b, ln2_g, ln2_b, b_proj, b_fc, b_qv, norms) = (
+        refs[:6], refs[6], refs[7:13], refs[13:22]
+    )
+    before, after, sems = refs[22:28], refs[28:34], refs[34]
+    parts = []
+    for i, v in enumerate(low):
+        parts += [(i, (e,)) for e in range(2)] if i < 2 else [(i, (...,))]
+
+    def load(n, i, at):
+        return pltpu.make_async_copy(low[i].at[at], before[i].at[at], sems.at[2 * n])
+
+    def store(n, i, at):
+        return pltpu.make_async_copy(after[i].at[at], wide[i].at[at], sems.at[2 * n + 1])
+
+    for n, (i, at) in enumerate(parts):
+        load(n, i, at).start()
+    for row, out in enumerate((b_out, ln1_g, ln1_b, ln2_g, ln2_b, b_proj, b_fc)):
+        out[...] = vec[row, :]
+    b_qv[...] = vec[7:9, : b_qv.shape[1]]
+    norms[...] = vec[9, :2]
+    for n, (i, at) in enumerate(parts):
+        load(n, i, at).wait()
+        after[i][at] = before[i][at].astype(F32)
+        store(n, i, at).start()
+    for n, (i, at) in enumerate(parts):
+        store(n, i, at).wait()
 
 
 def shards(
@@ -868,17 +956,24 @@
             V((8, D), F32),
             V((1, FH), F32),
             V((2, 16, D), F32),
+            V((QUAD, 8, 128), F32),
             V((QUAD, 16, D), F32),
             V((n_col, 16, D), F32),
-            V((3, 2, HQ, D), BF),
-            V((2, HQ, D), BF),
-            V((2, DH, FH), BF),
-            V((2, FQ, D), BF),
-            V((3, 3, 2, q48, D), BF),
-            V((3, 2, o48, D), BF),
-            V((3, 2, fa, FH), BF),
-            V((3, 2, fb, FH), BF),
+            V((3, 2, 2, 2, q48, D), BF),
+            V((2, 2, 2, o48, D), BF),
+            V((2, 2, 2, fa, FH), BF),
+            V((2, 2, 2, fb, FH), BF),
+            V((2, 2, 2, p192, D), BF),
             V((3, 2, p192, D), BF),
+            *[
+                V(shape, BF)
+                for shape in ((3, 2, 2, q48, D), (2, 2, o48, D), (2, 2, fa, FH), (2, 2, fb, FH))
+            ],
+            *[
+                V(shape, BF)
+                for _ in "OY"
+                for shape in ((3, 2, q48, D), (2, o48, D), (2, fa, FH), (2, fb, FH))
+            ],
             V((3, 2, q48, D), BF),
             V((2, o48, D), BF),
             V((2, fa, FH), BF),
@@ -899,8 +994,8 @@
             V((fa, FQ), BF),
             V((fb, FQ), BF),
             V((p192, DH), BF),
-            pltpu.SemaphoreType.DMA((200,)),
-            pltpu.SemaphoreType.DMA((200,)),
+            pltpu.SemaphoreType.DMA((240,)),
+            pltpu.SemaphoreType.DMA((240,)),
         ],
         compiler_params=pltpu.CompilerParams(
             collective_id=0, has_side_effects=True, vmem_limit_bytes=63 * 2**20
@@ -909,15 +1004,32 @@
         layer_in, cotangent, wq_t, w_out, w_fc, w_proj, b_fc, b_qv, lengths,
         b_out, ln1_g, ln1_b, ln2_g, ln2_b, b_proj,
     )
-    lo, gi, gq, go, gf, gp, vec = outs
-    norms = vec[9:11, 0]
-    lo, gi, gq, go, gf, gp = (v.astype(F32) for v in (lo, gi, gq, go, gf, gp))
+    low, vec = outs[:6], outs[6]
+    line = jax.ShapeDtypeStruct((D,), F32)
+    outs = pl.pallas_call(
+        widen,
+        name="widen",
+        out_shape=(
+            *(jax.ShapeDtypeStruct(v.shape, F32) for v in low),
+            *(line,) * 7,
+            jax.ShapeDtypeStruct((2, HQ), F32),
+            jax.ShapeDtypeStruct((2,), F32),
+        ),
+        in_specs=[anyspec] * 6 + [vm],
+        out_specs=(anyspec,) * 6 + (vm,) * 9,
+        scratch_shapes=[
+            *(V(v.shape, BF) for v in low), *(V(v.shape, F32) for v in low), pltpu.SemaphoreType.DMA((16,))
+        ],
+        compiler_params=pltpu.CompilerParams(vmem_limit_bytes=63 * 2**20),
+    )(*low, vec)
+    lo, gi, gq, go, gf, gp = outs[:6]
+    vec, norms = outs[6:14], outs[14]
     gq = jnp.transpose(gq, (2, 0, 1))
     if pairs > 1:
         groups = [[2 * p + q for p in range(pairs)] for q in range(2)]
         cores = [[2 * p, 2 * p + 1] for p in range(pairs)]
-        gq, go, gf, gp, vec = (
-            lax.psum(v, "row", axis_index_groups=groups) for v in (gq, go, gf, gp, vec)
+        gq, go, gf, gp, *vec = (
+            lax.psum(v, "row", axis_index_groups=groups) for v in (gq, go, gf, gp, *vec)
         )
 
         def share(v, axis):
@@ -926,11 +1038,8 @@
             return lax.dynamic_slice_in_dim(whole, r * part, part, axis)
 
         gq, go, gf, gp = share(gq, 0), share(go, 1), share(gf, 0), share(gp, 1)
-    return (
-        lo, gi, norms, gq, vec[7:9, :HQ], go,
-        vec[V_BOUT], vec[V_LN1G], vec[V_LN1B], vec[V_LN2G], vec[V_LN2B],
-        gf, vec[6], gp, vec[V_BPROJ],
-    )
+    gb_out, g1, b1, g2, b2, gb_proj, gb_fc, gb_qv = vec
+    return (lo, gi, norms, gq, gb_qv, go, gb_out, g1, b1, g2, b2, gf, gb_fc, gp, gb_proj)
 
 
 def solution(mesh):

time: 204 us -> 192 us (0.941)
  other arithmetic: 7.52 us -> 0 us
  local copies, waits for them, and re-layouts: 4.29 us -> 0 us
    convert_element_type x5 -> x0, other arithmetic: 6.55 us -> none  [shards(): lo, gi, gq, go, gf, gp = (v.astype(F32) for v in (lo, gi, gq, go, gf, gp))]
    pallas_call x1, Pallas kernels: 191 us -> 185 us  [shards(): pl.pallas_call(kernel, name='layer', out_shape=(jax.ShapeDtypeStruct((E,...]
    pallas_call x0 -> x1, Pallas kernels: none -> 5.4 us  [shards(): pl.pallas_call(widen, name='widen', out_shape=(*(jax.ShapeDtypeStruct(v.s...]
    slice x3 -> x0, local copies, waits for them, and re-layouts: 4.27 us -> none  [the longest x1 1.67 us: shards(): vec[V_BPROJ]]
where the time goes in v2:
time: 192 us; the launch traced here: 191 us
  Pallas kernels  190 us (99%)
    pallas_call x1, Pallas kernels, shards(): pl.pallas_call(kernel, name='layer', out_shape=(jax.ShapeDtypeStruct((E,...  185 us
    pallas_call x1, Pallas kernels, shards(): pl.pallas_call(widen, name='widen', out_shape=(*(jax.ShapeDtypeStruct(v.s...  5.4 us

profile of v2, /device:TPU:0, one launch (start us, length us, event | category | flops | bytes accessed | tf_op | source)
XLA Modules:
  0.0 191.1 jit_solution(16293216091339413557)
XLA Ops:
  0.7 184.9 %layer.1 = (bf16[2,256,768]{2,1,0:T(8,128)(2,1)}, bf16[2,256,768]{2,1,0:T(8,128)(2,1)}, bf16[3,192,384]{2,1,0:T(8,128)(2,1)}, bf16[192,384]{1,0:T(8,128)(2,1)}, ...) custom-call(f32[2,256,768]{2,1,0:T(8,128)} %x_in.1, f32[2,256,768]{2,1,0:T(8,128)} %cot_in.1, ...), custom_call_target="tpu_custom_call" | custom-call | tf_op jit(solution)/shard_map/layer/pallas_call | solution.py:910
  185.6 5.4 %widen.1 = (f32[2,256,768]{2,1,0:T(8,128)}, f32[2,256,768]{2,1,0:T(8,128)}, f32[3,192,384]{2,1,0:T(8,128)}, f32[192,384]{1,0:T(8,128)}, f32[384,768]{1,0:T(8,128...) custom-call(bf16[2,256,768]{2,1,0:T(8,128)(2,1)} %get-tuple-element., ...), custom_call_target="tpu_custom_call" | custom-call | tf_op jit(solution)/shard_map/widen/pallas_call | solution.py:1009

commit v3 on v2

--- a/solution.py
+++ b/solution.py
@@ -47,8 +47,8 @@
 def kernel(
     x_in, cot_in, wq_in, wo_in, wf_in, wp_in, bfc_in, bqv_in, len_in, b_out, ln1_g, ln1_b, ln2_g, ln2_b, b_proj,
     lo_out, gi_out, gq_out, go_out, gf_out, gp_out, vec_out,
-    XS, XH, CS, misc_in, XR, H, A1, WQ, WO, WF, WP, MISC, QKV, CTX, LSE, KB, ACC,
-    PS, PR, A2, M, SL, GF, GA, GCTX, GQKV, DK, DV, LO, GI,
+    XS, XH, CS, misc_in, XR, H, HG, A1, WQ, WO, WF, WP, MISC, QKV, CTX, LSE, KB, ACC,
+    PS, PR, A2, M, SL, GF, GA, GCTX, GQKV, DK, DV,
     V8, SQ, VF, VK, FAC, VP, VZ,
     GWQ, GWO, GWF, GWF2, GWP, RP, XQ, XO, XF, XF2, OQ, OO, OF, OF2, YQ, YO, YF, YF2, SQW, SOW, SFW, SFW2, SPW, BQ, BO, BF1, BF2, BP, UQ, UO, UF, UF2, UP, ZQ, ZO, ZF, ZF2, ZP, EQ, EO, EF, EF2, EP,
     ss, rs,
@@ -108,6 +108,11 @@
         when(cond, lambda: make().start())
         pending.append((cond, make))
 
+    def flush(count):
+        for cond, make in pending[:count]:
+            when(cond, lambda: make().wait_send())
+        del pending[:count]
+
     def local(src, dst, rsem, cond=True):
         when(cond, lambda: pltpu.make_async_copy(src(), dst(), rs.at[rsem]).start())
 
@@ -127,13 +132,14 @@
 
     barrier = pltpu.get_barrier_semaphore()
     line = [at(d, k, z ^ j) for j in (1, 2, 3)] + [at(d, 1 - k, z ^ j) for j in (0, 1, 2, 3)]
-    for dev in quad + line:
+    quad_mates = [at(d ^ j, 1 - k, z) for j in (1, 2, 3)]
+    for dev in quad + quad_mates + line:
         pl.semaphore_signal(barrier, inc=1, device_id=dev, device_id_type=MESH)
-    pl.semaphore_wait(barrier, len(quad) + len(line))
-
-    def line_send(src, dst, parts=(0, 1), base=None):
-        base = new_recv(2) if base is None else base
-        for i in parts:
+    pl.semaphore_wait(barrier, len(quad) + len(quad_mates) + len(line))
+
+    def line_send(src, dst):
+        base = new_recv(2)
+        for i in range(2):
             mine = (zk == k) & (2 * k + i == z)
             send(lambda i=i: src(i), lambda: dst(zs), base + zs, at(d, zk, 2 * k + i), jnp.logical_not(mine))
             local(lambda i=i: src(i), lambda: dst(zs), base + zs, mine)
@@ -397,12 +403,19 @@
     lax.fori_loop(0, HC // 128, attend, 0)
     w_proj2.hop()
 
-    def split_sum(n, product):
+    def split_other(n, product):
         base = new_recv(2)
         PS[n] = product(pl.ds(mo(other, 16), 2 * T)).astype(BF).reshape(2, T, D)
         for s in range(2):
             send(lambda s=s: PS.at[n, s], lambda s=s: PR.at[n, s], base + s, mate)
+        return base
+
+    def split_own(product):
         ACC[...] = product(pl.ds(mo(own, 16), 2 * T)).reshape(2, T, D)
+
+    def split_sum(n, product):
+        base = split_other(n, product)
+        split_own(product)
         return base
 
     def split_wait(n, base, s):
@@ -412,6 +425,7 @@
     ex = split_sum(0, lambda rows: dot(CTX[rows, :], WO[...]))
     w_proj.forward()
     cot_sem = send_cot()
+    sent = len(pending)
     a2_sem = new_recv(2)
     for s in range(2):
         split_wait(0, ex, s)
@@ -457,10 +471,6 @@
     hidden(own, first, FC - first)
     w_proj2.relay()
     hidden(other, first, FC - first)
-    w_proj.ready()
-    w_proj2.ready()
-    ex = split_sum(1, lambda rows: dot(M[rows, :], WP[...]))
-
     gf_sem = new_recv(2)
     for s in range(2):
         line_wait(lambda i: GF.at[pl.ds(mo(own + i * T, 16), T), :], cot_sem, s)
@@ -477,17 +487,10 @@
         mine = lambda s=s: GF.at[pl.ds(mo(own + s * T, 16), T), :]
         send(mine, mine, gf_sem + s, mate)
 
-    for s in range(2):
-        split_wait(1, ex, s)
-
-        def output_rows(i, c):
-            rows = rows_of(0, i, RB)
-            LO[s, rows, :] = (H[s, rows, :] + ACC[s, rows, :] + PR[1, s, rows, :].astype(F32) + b_proj).astype(BF)
-            return c
-
-        lax.fori_loop(0, T // RB, output_rows, 0)
-    lo_sem = line_send(lambda i: LO.at[i], lambda i: lo_out.at[i])
-
+    w_proj.ready()
+    w_proj2.ready()
+    mlp_rows = lambda rows: dot(M[rows, :], WP[...])
+    mlp_ex = split_other(1, mlp_rows)
     for s in range(2):
         arrive(lambda: GF.at[pl.ds(mo(other + s * T, 16), T), :], gf_sem + s)
 
@@ -562,9 +565,9 @@
             self.G, self.X, self.O, self.Y = G, X, O, Y
             self.raw, self.cross = new_recv(2), new_recv(2)
 
-        def spread(self):
-            send(lambda: self.G.at[0, :, 1 - bit[0]], lambda: self.X.at[0], self.raw, quad[0])
-            send(lambda: self.G.at[1, 1 - bit[1]], lambda: self.X.at[1], self.raw + 1, quad[1])
+        def spread(self, cond=True):
+            send(lambda: self.G.at[0, :, 1 - bit[0]], lambda: self.X.at[0], self.raw, quad[0], cond)
+            send(lambda: self.G.at[1, 1 - bit[1]], lambda: self.X.at[1], self.raw + 1, quad[1], cond)
 
         def scale(self):
             _, n, width = self.S.shape
@@ -667,13 +670,27 @@
                 - scaled * jnp.mean(through * scaled, axis=-1, keepdims=True)
             )
             V8[V_BOUT] += fold8(g)
-            H[s, rows, :] = g
+            HG[s, rows, :] = g
             GA[full, :] = g.astype(BF)
             return c
 
         lax.fori_loop(0, T // RB, second_back, 0)
         mine = lambda s=s: GA.at[pl.ds(mo(own + s * T, 16), T), :]
         send(mine, mine, ga_sem + s, mate)
+    split_own(mlp_rows)
+    flush(sent)
+    LO, GI = CS, XS
+    for s in range(2):
+        split_wait(1, mlp_ex, s)
+
+        def output_rows(i, c):
+            rows = rows_of(0, i, RB)
+            LO[s, rows, :] = (H[s, rows, :] + ACC[s, rows, :] + PR[1, s, rows, :].astype(F32) + b_proj).astype(BF)
+            return c
+
+        lax.fori_loop(0, T // RB, output_rows, 0)
+    lo_sem = line_send(lambda i: LO.at[i], lambda i: lo_out.at[i])
+
     for s in range(2):
         arrive(lambda: GA.at[pl.ds(mo(other + s * T, 16), T), :], ga_sem + s)
 
@@ -729,7 +746,7 @@
 
     ex = split_sum(3, grad_norm_in)
     grad_fc(GWF2, 128, FR - 128)
-    g_fc2.spread()
+    g_fc2.spread(k == 0)
     for s in range(2):
         split_wait(3, ex, s)
 
@@ -740,7 +757,7 @@
             through = up * ln1_g
             V8[V_LN1G] += fold8(up * scaled)
             V8[V_LN1B] += fold8(up)
-            g = H[s, rows, :] + inverse * (
+            g = HG[s, rows, :] + inverse * (
                 through
                 - jnp.mean(through, axis=-1, keepdims=True)
                 - scaled * jnp.mean(through * scaled, axis=-1, keepdims=True)
@@ -750,7 +767,8 @@
 
         lax.fori_loop(0, T // RB, first_back, 0)
 
-    gi_sem = line_send(lambda i: GI.at[i], lambda i: gi_out.at[i], (0,))
+    send_gi = lambda b: line_send(lambda i: GI.at[i, part_of(b)], lambda i: gi_out.at[i, part_of(b)])
+    gi_sems = [send_gi(0)]
 
     def grad_qkv(i, c):
         g = t_dot(GQKV[i], A1[...])
@@ -779,26 +797,31 @@
     FAC[dq] = jnp.broadcast_to(factor, (8, 128))
     fac_sem, vp_sem = new_recv(3), new_recv(3)
     for j in (1, 2, 3):
-        send(lambda: FAC.at[dq], lambda: FAC.at[dq], fac_sem + j - 1, quad[j - 1])
+        for dev in (quad[j - 1], quad_mates[j - 1]):
+            send(lambda: FAC.at[dq], lambda: FAC.at[dq], fac_sem + j - 1, dev, k == 1)
     VP[dq] = jnp.concatenate([pack, jnp.zeros((4, D), F32)], axis=0)
+    for j in (1, 2, 3):
+        arrive(lambda: FAC.at[dq ^ j], fac_sem + j - 1)
+
+    order = [g_proj, g_out, g_fc, g_fc2, *g_qkv]
+    g_proj.reduce()
+    g_out.scale()
+    g_fc.scale()
+    g_fc2.spread(k == 1)
     for part in g_qkv:
         part.spread()
-
-    for j in (1, 2, 3):
-        arrive(lambda: FAC.at[dq ^ j], fac_sem + j - 1)
-
-    order = [g_proj, g_out, g_fc, g_fc2, *g_qkv]
-    g_proj.reduce()
-    for part in order[1:]:
-        part.scale()
     for j in (1, 2, 3):
         send(lambda: VP.at[dq], lambda: VP.at[dq], vp_sem + j - 1, quad[j - 1])
     g_out.reduce()
     g_fc.reduce()
     g_proj.middle()
     g_out.middle()
+    g_fc.middle()
+    gi_sems.append(send_gi(1))
+    for part in (g_fc2, *g_qkv):
+        part.scale()
+    g_proj.finish()
     g_fc2.reduce()
-    g_fc.middle()
     for j in (1, 2, 3):
         arrive(lambda: VP.at[dq ^ j], vp_sem + j - 1)
     total = jnp.zeros((12, D), F32)
@@ -810,13 +833,11 @@
         send(lambda: VZ.at[z], lambda: VZ.at[z], vz_sem + j - 1, at(d, k, z ^ j))
     for part in g_qkv:
         part.reduce()
-    g_proj.finish()
-    g_fc2.middle()
     g_out.finish()
     g_fc.finish()
+    g_fc2.middle()
     for part in g_qkv:
         part.middle()
-    line_send(lambda i: GI.at[i], lambda i: gi_out.at[i], (1,), gi_sem)
     g_fc2.finish()
     for part in g_qkv:
         part.finish()
@@ -842,9 +863,9 @@
         part.done()
     for i in range(2):
         line_wait(lambda i: lo_out.at[i], lo_sem, i)
-        line_wait(lambda i: gi_out.at[i], gi_sem, i)
-    for cond, make in pending:
-        when(cond, lambda: make().wait_send())
+        for b in range(2):
+            line_wait(lambda i: gi_out.at[i, part_of(b)], gi_sems[b], i)
+    flush(len(pending))
 
 
 def widen(*refs):
@@ -928,6 +949,7 @@
             V((8, D), F32),
             V((2, T, D), BF),
             V((2, T, D), F32),
+            V((2, T, D), F32),
             V((L, D), BF),
             V((3, HC, D), BF),
             V((HC, D), BF),
@@ -950,8 +972,6 @@
             V((3, L, HC), BF),
             V((L, 128), F32),
             V((L, 128), F32),
-            V((2, T, D), BF),
-            V((2, T, D), BF),
             V((6, 8, D), F32),
             V((8, D), F32),
             V((1, FH), F32),

time: 192 us -> 190 us (0.990)
  Pallas kernels: 190 us -> 187 us
    pallas_call x1, Pallas kernels: 185 us -> 182 us  [shards(): pl.pallas_call(kernel, name='layer', out_shape=(jax.ShapeDtypeStruct((E,...]
where the time goes in v3:
time: 190 us; the launch traced here: 188 us
  Pallas kernels  187 us (98%)
    pallas_call x1, Pallas kernels, shards(): pl.pallas_call(kernel, name='layer', out_shape=(jax.ShapeDtypeStruct((E,...  182 us
    pallas_call x1, Pallas kernels, shards(): pl.pallas_call(widen, name='widen', out_shape=(*(jax.ShapeDtypeStruct(v.s...  5.4 us

profile of v3, /device:TPU:0, one launch (start us, length us, event | category | flops | bytes accessed | tf_op | source)
XLA Modules:
  0.0 188.0 jit_solution(9911651044881249424)
XLA Ops:
  0.7 181.8 %layer.1 = (bf16[2,256,768]{2,1,0:T(8,128)(2,1)}, bf16[2,256,768]{2,1,0:T(8,128)(2,1)}, bf16[3,192,384]{2,1,0:T(8,128)(2,1)}, bf16[192,384]{1,0:T(8,128)(2,1)}, ...) custom-call(f32[2,256,768]{2,1,0:T(8,128)} %x_in.1, f32[2,256,768]{2,1,0:T(8,128)} %cot_in.1, ...), custom_call_target="tpu_custom_call" | custom-call | tf_op jit(solution)/shard_map/layer/pallas_call | solution.py:931
  182.5 5.4 %widen.1 = (f32[2,256,768]{2,1,0:T(8,128)}, f32[2,256,768]{2,1,0:T(8,128)}, f32[3,192,384]{2,1,0:T(8,128)}, f32[192,384]{1,0:T(8,128)}, f32[384,768]{1,0:T(8,128...) custom-call(bf16[2,256,768]{2,1,0:T(8,128)(2,1)} %get-tuple-element., ...), custom_call_target="tpu_custom_call" | custom-call | tf_op jit(solution)/shard_map/widen/pallas_call | solution.py:1029

commit v4 on v3

--- a/solution.py
+++ b/solution.py
@@ -366,11 +366,11 @@
 
     between = {
         (0, 3): (w_out.hop, w_fc2.push),
-        (1, 0): (w_fc.hop,),
-        (1, 2): (w_out.forward, w_proj.push),
-        (1, 3): (w_fc.forward, w_fc2.hop),
-        (2, 0): (w_out.relay, w_proj2.push),
-        (2, 2): (w_fc.relay, w_proj.hop),
+        (1, 0): (w_fc.hop, w_proj.push),
+        (1, 2): (w_out.forward,),
+        (1, 3): (w_fc.forward, w_fc2.hop, w_proj2.push),
+        (2, 0): (w_out.relay, w_proj.hop),
+        (2, 2): (w_fc.relay,),
         (2, 3): (w_fc2.forward,),
     }
 
@@ -402,6 +402,8 @@
 
     lax.fori_loop(0, HC // 128, attend, 0)
     w_proj2.hop()
+    cot_sem = send_cot()
+    sent = len(pending)
 
     def split_other(n, product):
         base = new_recv(2)
@@ -424,8 +426,6 @@
     w_out.ready()
     ex = split_sum(0, lambda rows: dot(CTX[rows, :], WO[...]))
     w_proj.forward()
-    cot_sem = send_cot()
-    sent = len(pending)
     a2_sem = new_recv(2)
     for s in range(2):
         split_wait(0, ex, s)
@@ -534,18 +534,24 @@
 
     class DirectPart(Part):
         def setup(self, G, R):
-            self.G, self.R, self.raw = G, R, new_recv(3)
+            self.G, self.R, self.raw = G, R, new_recv(6)
 
         def quarter(self, q):
             return self.G.at[:, q // 2, lax.rem(q, 2)]
 
-        def spread(self):
+        def spread(self, a):
             for j in (1, 2, 3):
-                send(lambda j=j: self.quarter(dq ^ j), lambda j=j: self.R.at[j - 1], self.raw + j - 1, quad[j - 1])
+                send(
+                    lambda j=j: self.G.at[a, (dq ^ j) // 2, lax.rem(dq ^ j, 2)],
+                    lambda j=j: self.R.at[j - 1, a],
+                    self.raw + 2 * j - 2 + a,
+                    quad[j - 1],
+                )
 
         def reduce(self):
             for j in (1, 2, 3):
-                arrive(lambda: self.R.at[j - 1], self.raw + j - 1)
+                for a in range(2):
+                    arrive(lambda: self.R.at[j - 1, a], self.raw + 2 * j - 2 + a)
             G, (_, n, width) = self.quarter(dq), self.S.shape
             factors, steps = wide_factors(QUAD, width), n // 16
 
@@ -613,8 +619,8 @@
             lambda q: gf_out.at[pl.ds(mo(start + q * n, 16), n), :],
         )
 
-    g_fc = fc_grad((GWF, XF, OF, YF), SFW, BF1, UF, ZF, EF, 0, 128 // QUAD)
-    g_fc2 = fc_grad((GWF2, XF2, OF2, YF2), SFW2, BF2, UF2, ZF2, EF2, 128, (FR - 128) // QUAD)
+    g_fc2 = fc_grad((GWF, XF, OF, YF), SFW, BF1, UF, ZF, EF, 0, 128 // QUAD)
+    g_fc = fc_grad((GWF2, XF2, OF2, YF2), SFW2, BF2, UF2, ZF2, EF2, 128, (FR - 128) // QUAD)
 
     def qkv_grad(i):
         return CrossPart(
@@ -634,8 +640,9 @@
         GWP[i // 2, lax.rem(i, 2)] = g.astype(BF).reshape(2, p192, D)
         return c
 
-    lax.fori_loop(0, 4, grad_proj, 0)
-    g_proj.spread()
+    for a in range(2):
+        lax.fori_loop(2 * a, 2 * a + 2, grad_proj, 0)
+        g_proj.spread(a)
 
     NB = 512
     NN = FH // NB
@@ -706,7 +713,7 @@
         SQ[...] += q[:, :D] + q[:, D:]
         G[...] = g.astype(BF).reshape(2, 2, 2, n // QUAD, FH)
 
-    grad_fc(GWF, 0, 128)
+    grad_fc(GWF2, 128, FR - 128)
     g_fc.spread()
 
     def attend_back(p):
@@ -745,7 +752,7 @@
         return dot(GQKV[0, rows, :], WQ[0]) + dot(GQKV[1, rows, :], WQ[1]) + dot(GQKV[2, rows, :], WQ[2])
 
     ex = split_sum(3, grad_norm_in)
-    grad_fc(GWF2, 128, FR - 128)
+    grad_fc(GWF, 0, 128)
     g_fc2.spread(k == 0)
     for s in range(2):
         split_wait(3, ex, s)
@@ -767,7 +774,8 @@
 
         lax.fori_loop(0, T // RB, first_back, 0)
 
-    send_gi = lambda b: line_send(lambda i: GI.at[i, part_of(b)], lambda i: gi_out.at[i, part_of(b)])
+    batches = [pl.ds(0, T // 2), pl.ds(T // 2, T // 4), pl.ds(3 * T // 4, T // 4)]
+    send_gi = lambda b: line_send(lambda i: GI.at[i, batches[b]], lambda i: gi_out.at[i, batches[b]])
     gi_sems = [send_gi(0)]
 
     def grad_qkv(i, c):
@@ -838,6 +846,7 @@
     g_fc2.middle()
     for part in g_qkv:
         part.middle()
+    gi_sems.append(send_gi(2))
     g_fc2.finish()
     for part in g_qkv:
         part.finish()
@@ -863,16 +872,14 @@
         part.done()
     for i in range(2):
         line_wait(lambda i: lo_out.at[i], lo_sem, i)
-        for b in range(2):
-            line_wait(lambda i: gi_out.at[i, part_of(b)], gi_sems[b], i)
+        for b in range(3):
+            line_wait(lambda i: gi_out.at[i, batches[b]], gi_sems[b], i)
     flush(len(pending))
 
 
 def widen(*refs):
-    low, vec, wide, (b_out, ln1_g, ln1_b, ln2_g, ln2_b, b_proj, b_fc, b_qv, norms) = (
-        refs[:6], refs[6], refs[7:13], refs[13:22]
-    )
-    before, after, sems = refs[22:28], refs[28:34], refs[34]
+    low, vec_in, wide, lines, b_qv, norms = refs[:6], refs[6], refs[7:13], refs[13:20], refs[20], refs[21]
+    before, after, vec, rows, sems, line_sems = refs[22:28], refs[28:34], refs[34], refs[35:42], refs[42], refs[43]
     parts = []
     for i, v in enumerate(low):
         parts += [(i, (e,)) for e in range(2)] if i < 2 else [(i, (...,))]
@@ -883,18 +890,27 @@
     def store(n, i, at):
         return pltpu.make_async_copy(after[i].at[at], wide[i].at[at], sems.at[2 * n + 1])
 
+    def store_line(i):
+        return pltpu.make_async_copy(rows[i], lines[i], line_sems.at[i])
+
+    load_vec = pltpu.make_async_copy(vec_in, vec, line_sems.at[7])
     for n, (i, at) in enumerate(parts):
         load(n, i, at).start()
-    for row, out in enumerate((b_out, ln1_g, ln1_b, ln2_g, ln2_b, b_proj, b_fc)):
-        out[...] = vec[row, :]
-    b_qv[...] = vec[7:9, : b_qv.shape[1]]
-    norms[...] = vec[9, :2]
+    load_vec.start()
     for n, (i, at) in enumerate(parts):
         load(n, i, at).wait()
         after[i][at] = before[i][at].astype(F32)
         store(n, i, at).start()
+    load_vec.wait()
+    for i in range(7):
+        rows[i][...] = vec[i, :]
+        store_line(i).start()
+    b_qv[...] = vec[7:9, : b_qv.shape[1]]
+    norms[...] = vec[9, :2]
     for n, (i, at) in enumerate(parts):
         store(n, i, at).wait()
+    for i in range(7):
+        store_line(i).wait()
 
 
 def shards(
@@ -1014,8 +1030,8 @@
             V((fa, FQ), BF),
             V((fb, FQ), BF),
             V((p192, DH), BF),
-            pltpu.SemaphoreType.DMA((240,)),
-            pltpu.SemaphoreType.DMA((240,)),
+            pltpu.SemaphoreType.DMA((264,)),
+            pltpu.SemaphoreType.DMA((264,)),
         ],
         compiler_params=pltpu.CompilerParams(
             collective_id=0, has_side_effects=True, vmem_limit_bytes=63 * 2**20
@@ -1035,10 +1051,14 @@
             jax.ShapeDtypeStruct((2, HQ), F32),
             jax.ShapeDtypeStruct((2,), F32),
         ),
-        in_specs=[anyspec] * 6 + [vm],
-        out_specs=(anyspec,) * 6 + (vm,) * 9,
+        in_specs=[anyspec] * 7,
+        out_specs=(anyspec,) * 13 + (vm,) * 2,
         scratch_shapes=[
-            *(V(v.shape, BF) for v in low), *(V(v.shape, F32) for v in low), pltpu.SemaphoreType.DMA((16,))
+            *(V(v.shape, BF) for v in low),
+            *(V(v.shape, F32) for v in (*low, vec)),
+            *[V((D,), F32)] * 7,
+            pltpu.SemaphoreType.DMA((16,)),
+            pltpu.SemaphoreType.DMA((8,)),
         ],
         compiler_params=pltpu.CompilerParams(vmem_limit_bytes=63 * 2**20),
     )(*low, vec)

time: 190 us -> 189 us (level)
  no operation moved by 1% of the time
where the time goes in v4:
time: 189 us
  Pallas kernels  188 us (99%)
    pallas_call x1, Pallas kernels, shards(): pl.pallas_call(kernel, name='layer', out_shape=(jax.ShapeDtypeStruct((E,...  183 us
    pallas_call x1, Pallas kernels, shards(): pl.pallas_call(widen, name='widen', out_shape=(*(jax.ShapeDtypeStruct(v.s...  4.65 us

profile of v4, /device:TPU:0, one launch (start us, length us, event | category | flops | bytes accessed | tf_op | source)
XLA Modules:
  0.0 188.7 jit_solution(8319264347463053445)
XLA Ops:
  0.7 183.2 %layer.1 = (bf16[2,256,768]{2,1,0:T(8,128)(2,1)}, bf16[2,256,768]{2,1,0:T(8,128)(2,1)}, bf16[3,192,384]{2,1,0:T(8,128)(2,1)}, bf16[192,384]{1,0:T(8,128)(2,1)}, ...) custom-call(f32[2,256,768]{2,1,0:T(8,128)} %x_in.1, f32[2,256,768]{2,1,0:T(8,128)} %cot_in.1, ...), custom_call_target="tpu_custom_call" | custom-call | tf_op jit(solution)/shard_map/layer/pallas_call | solution.py:947
  183.9 4.7 %widen.1 = (f32[2,256,768]{2,1,0:T(8,128)}, f32[2,256,768]{2,1,0:T(8,128)}, f32[3,192,384]{2,1,0:T(8,128)}, f32[192,384]{1,0:T(8,128)}, f32[384,768]{1,0:T(8,128...) custom-call(bf16[2,256,768]{2,1,0:T(8,128)(2,1)} %get-tuple-element., ...), custom_call_target="tpu_custom_call" | custom-call | tf_op jit(solution)/shard_map/widen/pallas_call | solution.py:1045

commit v5 on v4

--- a/solution.py
+++ b/solution.py
@@ -293,7 +293,7 @@
     w_qkv.forward()
     w_qkv.relay()
 
-    RB = 128
+    RB = 256
     a1_sem = new_recv(2)
 
     def rows_of(base, i, n):

time: 189 us -> 188 us (level)
  no operation moved by 1% of the time
where the time goes in v5:
time: 188 us; the launch traced here: 187 us
  Pallas kernels  187 us (99%)
    pallas_call x1, Pallas kernels, shards(): pl.pallas_call(kernel, name='layer', out_shape=(jax.ShapeDtypeStruct((E,...  182 us
    pallas_call x1, Pallas kernels, shards(): pl.pallas_call(widen, name='widen', out_shape=(*(jax.ShapeDtypeStruct(v.s...  4.65 us

profile of v5, /device:TPU:0, one launch (start us, length us, event | category | flops | bytes accessed | tf_op | source)
XLA Modules:
  0.0 187.5 jit_solution(9611296908844154119)
XLA Ops:
  0.7 182.0 %layer.1 = (bf16[2,256,768]{2,1,0:T(8,128)(2,1)}, bf16[2,256,768]{2,1,0:T(8,128)(2,1)}, bf16[3,192,384]{2,1,0:T(8,128)(2,1)}, bf16[192,384]{1,0:T(8,128)(2,1)}, ...) custom-call(f32[2,256,768]{2,1,0:T(8,128)} %x_in.1, f32[2,256,768]{2,1,0:T(8,128)} %cot_in.1, ...), custom_call_target="tpu_custom_call" | custom-call | tf_op jit(solution)/shard_map/layer/pallas_call | solution.py:947
  182.6 4.7 %widen.1 = (f32[2,256,768]{2,1,0:T(8,128)}, f32[2,256,768]{2,1,0:T(8,128)}, f32[3,192,384]{2,1,0:T(8,128)}, f32[192,384]{1,0:T(8,128)}, f32[384,768]{1,0:T(8,128...) custom-call(bf16[2,256,768]{2,1,0:T(8,128)(2,1)} %get-tuple-element., ...), custom_call_target="tpu_custom_call" | custom-call | tf_op jit(solution)/shard_map/widen/pallas_call | solution.py:1045
